TPU v7x, 32 devices: a whole 2x2x4 slice. The times are simulated.
32 devices in a mesh: groups: 2 (over y), down: 4 (over z), cross: 2 (over x), depth: 2 (over core).
Axes of the slice: x: 2, y: 2, z: 4, core: 2. Of those that a mesh axis runs over, the one named last changes fastest.
Arguments:
- positions: float32 [3, 16, 4, 4, 128], P(None, ('groups', 'down'), 'cross', 'depth'), parts along dimension 1, may hold values from -0.5 to 0.5
- velocities: float32 [3, 16, 4, 4, 128], P(None, ('groups', 'down'), 'cross', 'depth'), parts along dimension 1, may hold values from -6 to 6
- sphere_radii: float32 [16, 4, 4, 128], P(('groups', 'down'), 'cross', 'depth'), parts along dimension 0, may hold values from 0.08 to 0.12
- counts: int32 [16, 4, 4], P(('groups', 'down'), 'cross', 'depth'), parts along dimension 0, may hold values from 32 to 128, as said below
- coefficients: float32 [48], replicated, may hold values from -0.6 to 0.6
Outputs:
- velocity_new: float32 [3, 16, 4, 4, 128], P(None, ('groups', 'down'), 'cross', 'depth'), parts along dimension 1
- contact_force: float32 [3, 16, 4, 4, 128], P(None, ('groups', 'down'), 'cross', 'depth'), parts along dimension 1
- residual_field: float32 [16, 4, 4], P(('groups', 'down'), 'cross', 'depth'), parts along dimension 0
- gram_matrix: float32 [96, 48], P('groups'), parts along dimension 0
- moment_vector: float32 [96], P('groups'), parts along dimension 0
There are 2 independent parts, one for each index of `groups`. A program takes and returns all parts, laid end to end along the dimension named above; an argument that names none is the same for every part. Nothing has to cross between parts.
Inputs may be any that keep to these rules, and one draw needn't show every extreme that they name: `counts`: slots 0 to count - 1 of a cell hold spheres, the rest are padding; every cell of the bottom depth layer holds 128.
All inputs are finite; a program needn't handle non-finite values.
Results may differ from a plain program's by a relative error of at most 0.0003.
Values sent between devices are 32-bit elements; how exact they have to be, the bound alone decides.
No kernel may reach another device: no remote copies, remote signals or barrier semaphores. Data moves between devices by JAX's collectives and lax.ppermute only.
A program may use at most 128 MiB of HBM per device.

v0:
```python
import functools

import jax
import jax.numpy as jnp
from jax import lax
from jax.experimental import pallas as pl
from jax.experimental.pallas import tpu as pltpu
from jax.sharding import PartitionSpec as P

STIFFNESS = 100.0
DAMPING = 20.0
TIME_STEP = 0.05
KERNEL_WIDTH = 0.4
KERNEL_NORM = 64.0
SOFTENING = 0.0001
RADIUS_REF = 0.1
MASS_SHIFT = 0.1
DEAD = -1000.0
TERMS = 48
S = 128
F32 = jnp.float32
BF16 = jnp.bfloat16
CELLS = tuple((a, b, z) for a in range(2) for b in range(2) for z in range(2))
PAIRS = ((0, 2), (4, 6), (1, 3), (5, 7))
PAIR_LIST = ((0, 0), (0, 1), (0, 2), (1, 1), (1, 2), (2, 2))
VMEM_SPEC = pl.BlockSpec(memory_space=pltpu.VMEM)
SMEM_SPEC = pl.BlockSpec(memory_space=pltpu.SMEM)
VMEM_LIMIT = 48 * 1024 * 1024


def row_ids(shape):
    return lax.broadcasted_iota(jnp.int32, shape, 0)


def lane_ids(shape):
    return lax.broadcasted_iota(jnp.int32, shape, 1)


def one_hot(condition):
    return jnp.where(condition, 1.0, 0.0).astype(BF16)


def split(value):
    high = value.astype(BF16)
    return high, value - high.astype(F32)


def matmul(left, right):
    return lax.dot_general(left, right, (((1,), (0,)), ((), ())), preferred_element_type=F32)


def matmul_turned(left, right):
    return lax.dot_general(left, right, (((1,), (1,)), ((), ())), preferred_element_type=F32)


def lane_gather(table, index):
    return jnp.take_along_axis(table, index, axis=1)


def pack_kernel(
    counts, positions_hbm, velocities_hbm, radii_hbm, own, inner, positions, velocities, radii, arrived
):
    copies = [
        pltpu.make_async_copy(source, target, arrived.at[k])
        for k, (source, target) in enumerate(
            ((positions_hbm, positions), (velocities_hbm, velocities), (radii_hbm, radii))
        )
    ]
    for copy in copies:
        copy.start()
    for copy in copies:
        copy.wait()
    depth = lax.axis_index("depth")
    lanes = lane_ids((1, S))
    for c, (a, b, z) in enumerate(CELLS):
        for k in range(3):
            own[c * 8 + k : c * 8 + k + 1, :] = positions[k, a, b, z : z + 1, :]
            own[c * 8 + 3 + k : c * 8 + 4 + k, :] = velocities[k, a, b, z : z + 1, :]
        live = lanes < counts[a, b, z]
        own[c * 8 + 6 : c * 8 + 7, :] = jnp.where(live, radii[a, b, z : z + 1, :], DEAD)
        own[c * 8 + 7 : c * 8 + 8, :] = jnp.zeros((1, S), F32)
    for column in range(4):
        source = pl.multiple_of(column * 16 + (1 - depth) * 8, 8)
        inner[column * 8 : column * 8 + 8, :] = own[pl.ds(source, 8), :]


def local_state(raw, centre):
    rows = row_ids(raw.shape)
    shift = jnp.where(rows == 0, centre[0], jnp.where(rows == 1, centre[1], centre[2]))
    return jnp.where(rows < 3, raw + shift, raw)


def piece_reader(refs, wide, height):
    own, depth_halo = refs[0], refs[1]
    x_before, x_after = refs[-2], refs[-1]

    def read(ref, cell):
        return ref[cell * height : cell * height + height, :]

    def cell(x, y, slot):
        if x in (0, 3):
            face = x_before if x == 0 else x_after
            if y in (1, 2):
                return read(face, (y - 1) * 2 + slot if slot < 2 else 4 + y - 1)
            side = 0 if y == 0 else 1
            return read(face, 6 + side * 2 + slot if slot < 2 else 10 + side)
        a = x - 1
        if y in (1, 2):
            return read(own, a * 4 + (y - 1) * 2 + slot) if slot < 2 else read(depth_halo, a * 2 + y - 1)
        if wide:
            before, after, diag_before, diag_after = refs[2:6]
            if slot < 2:
                return read(before if y == 0 else after, a * 2 + slot)
            return read(diag_before if y == 0 else diag_after, a)
        side, diag = refs[2:4]
        b = 1 if y == 0 else 0
        return read(side, a * 4 + b * 2 + slot) if slot < 2 else read(diag, a * 2 + b)

    return cell


def own_place(a, b, z):
    return ((a + 1) * 4 + b + 1) * 3 + z


def extended_cells(depth):
    halo_z = 1.5 - 3.0 * depth.astype(F32)
    for x in range(4):
        for y in range(4):
            for slot in range(3):
                centre = (x - 1.5, y - 1.5, slot - 0.5 if slot < 2 else halo_z)
                yield x, y, slot, ((x * 4 + y) * 3 + slot) * 8, centre


def contact_scratch(width):
    return [
        pltpu.VMEM((48 * 8, S), F32),
        pltpu.VMEM((8 * 48, S), jnp.int32),
        pltpu.VMEM((8 * 48, S), jnp.int32),
        pltpu.VMEM((8 * 48, S), jnp.int32),
        pltpu.VMEM((8 * 48, S), jnp.int32),
        pltpu.VMEM((8, 27, 8, S), F32),
        pltpu.VMEM((8, 7, S, S), F32),
        pltpu.VMEM((8, width, S, S), F32),
    ]


def contact_all(depth, width, scratch):
    local_ref, index_ref, base_ref, amount_ref, chosen_ref, list_ref, spread_ref, sum_ref = scratch
    inner = 1 - depth
    for c, (a, b, z) in enumerate(CELLS):
        start = own_place(a, b, z) * 8
        turned = jnp.transpose(local_ref[start : start + 8, :])
        for k in range(7):
            spread_ref[c, k] = jnp.broadcast_to(turned[:, k : k + 1], (S, S))

    place = [local_ref[pl.ds(k, 48, stride=8), :] for k in range(3)]
    radius = local_ref[pl.ds(6, 48, stride=8), :]
    rows = row_ids((48, S))
    row_x, row_y, row_slot = rows // 12, (rows // 3) % 4, rows % 3
    masks = []
    for a, b, z in CELLS:
        start = own_place(a, b, z) * 8
        mine = local_ref[start : start + 8, :]
        live = mine[6:7] > 0.0
        low = jnp.min(jnp.where(live, mine, 1e9), axis=1, keepdims=True)
        high = jnp.max(jnp.where(live, mine, -1e9), axis=1, keepdims=True)
        reach = radius + high[6:7]
        near = jnp.logical_and(
            jnp.logical_and(row_x >= a, row_x <= a + 2), jnp.logical_and(row_y >= b, row_y <= b + 2)
        )
        near = jnp.logical_and(near, jnp.logical_or(row_slot < 2, inner == z))
        for k in range(3):
            near = jnp.logical_and(near, place[k] + reach > low[k : k + 1])
            near = jnp.logical_and(near, place[k] - reach < high[k : k + 1])
        masks.append(jnp.where(near, 1.0, 0.0).astype(F32))
    mask = jnp.concatenate(masks, axis=0).astype(BF16)
    upper = one_hot(row_ids((S, 2 * S)) <= lane_ids((S, 2 * S)))
    sums = matmul(mask, upper)
    prefix, amount = sums[:, :S], sums[:, S:]
    before = one_hot(lane_ids((48, 48)) < row_ids((48, 48)))
    totals = []
    for c in range(8):
        part = amount[c * 48 : c * 48 + 48]
        base = matmul(before, part.astype(BF16))
        base_ref[c * 48 : c * 48 + 48, :] = base.astype(jnp.int32)
        totals.append((base[47:48, 0:1] + part[47:48, 0:1]).astype(jnp.int32)[0, 0])
    amount_ref[...] = amount.astype(jnp.int32)
    wanted = lane_ids((8 * 48, S)).astype(F32)
    index = jnp.zeros((8 * 48, S), jnp.int32)
    for step in (64, 32, 16, 8, 4, 2, 1):
        probe = lane_gather(prefix, index + (step - 1))
        index = jnp.where(probe <= wanted, index + step, index)
    index_ref[...] = index
    tiles = [(total + (S - 1)) // S for total in totals]
    most = tiles[0]
    for count in tiles[1:]:
        most = jnp.maximum(most, count)

    empty = jnp.where(row_ids((8, S)) == 6, DEAD, 0.0).astype(F32)

    def gather_tiles(t, carry):
        want = t * S + lane_ids((8 * 48, S)) - base_ref[...]
        valid = jnp.logical_and(want >= 0, want < amount_ref[...])
        source = lane_gather(index_ref[...], jnp.clip(want, 0, S - 1))
        chosen_ref[...] = jnp.where(valid, source, -1)
        for c, (a, b, z) in enumerate(CELLS):
            tile = empty
            for dx in range(3):
                for dy in range(3):
                    for slot in range(3):
                        n = ((a + dx) * 4 + b + dy) * 3 + slot
                        pick = jnp.broadcast_to(chosen_ref[c * 48 + n : c * 48 + n + 1, :], (8, S))
                        values = lane_gather(local_ref[n * 8 : n * 8 + 8, :], jnp.maximum(pick, 0))
                        tile = jnp.where(pick >= 0, values, tile)
            list_ref[c, t] = tile
        return carry

    gather_tiles(0, 0)
    lax.fori_loop(1, most, gather_tiles, 0)

    def pair_tile(c, t, first):
        tile = list_ref[c, t]
        other = [jnp.broadcast_to(tile[k : k + 1], (8, S)) for k in range(7)]
        for block in range(16):
            row = block * 8
            me = [spread_ref[c, k, row : row + 8, :] for k in range(7)]
            r = [me[k] - other[k] for k in range(3)]
            u = [me[3 + k] - other[3 + k] for k in range(3)]
            squared = r[0] * r[0] + r[1] * r[1] + r[2] * r[2] + SOFTENING
            inverse = lax.rsqrt(squared)
            along = u[0] * r[0] + u[1] * r[1] + u[2] * r[2]
            overlap = jnp.maximum((me[6] + other[6]) * inverse - 1.0, 0.0)
            weight = overlap * (STIFFNESS - (DAMPING * along) * inverse)
            terms = [weight * r[k] for k in range(3)]
            if width == 9:
                terms += [terms[left] * r[right] for left, right in PAIR_LIST]
            for k, term in enumerate(terms):
                if first:
                    sum_ref[c, k, row : row + 8, :] = term
                else:
                    sum_ref[c, k, row : row + 8, :] += term

    for c in range(8):
        pair_tile(c, 0, True)
    for group in PAIRS:

        def later_tile(t, carry):
            for c in group:
                pair_tile(c, t, False)
            return carry

        lax.fori_loop(1, jnp.maximum(tiles[group[0]], tiles[group[1]]), later_tile, 0)
    lanes = lane_ids((S, S))
    table = jnp.zeros((S, S), F32)
    for k in range(width):
        for c in range(8):
            column = jnp.sum(sum_ref[c, k], axis=1, keepdims=True)
            table = jnp.where(lanes == k * 8 + c, column, table)
    return jnp.transpose(table)[0 : width * 8]


def mass_of(radius):
    scaled = radius / RADIUS_REF
    return scaled * scaled * scaled


def step_kernel(wide, *refs):
    count = 8 if wide else 6
    pieces, (velocity_out, own_out, inner_out) = refs[:count], refs[count : count + 3]
    scratch = refs[count + 3 :]
    own = pieces[0]
    depth = lax.axis_index("depth")
    cell = piece_reader(pieces, wide, 8)
    for x, y, slot, start, centre in extended_cells(depth):
        scratch[0][start : start + 8, :] = local_state(cell(x, y, slot), centre)
    sums = contact_all(depth, 3, scratch)
    radius = own[pl.ds(6, 8, stride=8), :]
    safe_mass = jnp.where(radius > 0.0, mass_of(radius), 1.0)
    for k in range(3):
        velocity = own[pl.ds(3 + k, 8, stride=8), :] + TIME_STEP * sums[k * 8 : k * 8 + 8] / safe_mass
        for c, (a, b, z) in enumerate(CELLS):
            own_out[c * 4 + k : c * 4 + k + 1, :] = velocity[c : c + 1]
            if z == 0:
                velocity_out[k, a, b, :, :] = velocity[c : c + 2]
    for c in range(8):
        own_out[c * 4 + 3 : c * 4 + 4, :] = jnp.zeros((1, S), F32)
    for column in range(4):
        chosen = own_out[column * 8 : column * 8 + 8, :]
        inner_out[column * 4 : column * 4 + 4, :] = jnp.where(depth == 0, chosen[4:8], chosen[0:4])


def field_kernel(wide, grid, *refs):
    count = 8 if wide else 6
    pieces, speeds = refs[:count], refs[count : 2 * count]
    force_out, node_out = refs[2 * count : 2 * count + 2]
    moment_ref = refs[2 * count + 2]
    scratch = refs[2 * count + 3 :]
    local_ref = scratch[0]
    depth = lax.axis_index("depth")
    down = lax.axis_index("down")
    cross = lax.axis_index("cross")
    cell = piece_reader(pieces, wide, 8)
    speed = piece_reader(speeds, wide, 4)
    for x, y, slot, start, centre in extended_cells(depth):
        old = cell(x, y, slot)
        new = speed(x, y, slot)[0:3]
        shift = jnp.where(
            row_ids((3, S)) == 0, centre[0], jnp.where(row_ids((3, S)) == 1, centre[1], centre[2])
        )
        local_ref[start : start + 3, :] = (old[0:3] + TIME_STEP * new) + shift
        local_ref[start + 3 : start + 6, :] = new
        local_ref[start + 6 : start + 8, :] = old[6:8]
    sums = contact_all(depth, 9, scratch)
    radius = pieces[0][pl.ds(6, 8, stride=8), :]
    mass = jnp.where(radius > 0.0, mass_of(radius), 0.0)
    moments = [mass] + [mass * speeds[0][pl.ds(k, 8, stride=4), :] for k in range(3)]
    moments += [0.5 * sums[k * 8 : k * 8 + 8] for k in range(3, 9)]
    moment_ref[...] = jnp.zeros((16, 8 * S), F32)
    for k in range(3):
        for c, (a, b, z) in enumerate(CELLS):
            if z == 0:
                force_out[k, a, b, :, :] = sums[k * 8 + c : k * 8 + c + 2]
    for m, moment in enumerate(moments):
        for c in range(8):
            moment_ref[m : m + 1, c * S : (c + 1) * S] = moment[c : c + 1]
    rows = row_ids((64, S))
    near_x, near_y, near_z = rows // 16 - 1, (rows // 4) % 4 - 1, rows % 4 - 1
    centres = [index.astype(F32) - 0.5 for index in (near_x, near_y, near_z)]
    kernels = []
    for a, b, z in CELLS:
        start = own_place(a, b, z) * 8
        squared = jnp.zeros((64, S), F32)
        for k in range(3):
            gap = local_ref[start + k : start + k + 1, :] - centres[k]
            squared = squared + gap * gap
        kernel = jnp.exp(squared * (-0.5 / (KERNEL_WIDTH * KERNEL_WIDTH))) / KERNEL_NORM
        beside = jnp.logical_and(
            jnp.logical_and(jnp.abs(near_x - a) <= 1, jnp.abs(near_y - b) <= 1),
            jnp.abs(near_z - z) <= 1,
        )
        kernels.append(jnp.where(beside, kernel, 0.0))
    kernel_high, kernel_low = split(jnp.concatenate(kernels, axis=1))
    moment_high, moment_low = split(moment_ref[...])
    wide_part = matmul_turned(
        jnp.concatenate([moment_high, moment_low.astype(BF16)], axis=0), kernel_high
    )
    near = wide_part[0:16] + wide_part[16:32] + matmul_turned(moment_high, kernel_low.astype(BF16))
    size_x, size_y, size_z = grid
    nodes = size_x * size_y * size_z
    lanes = lane_ids((64, nodes))
    row = row_ids((64, nodes))
    target_x = (down * 2 + row // 16 - 1 + size_x) % size_x
    target_y = (cross * 2 + (row // 4) % 4 - 1 + size_y) % size_y
    target_z = depth * 2 + row % 4 - 1
    inside = jnp.logical_and(target_z >= 0, target_z < size_z)
    target = (target_x * size_y + target_y) * size_z + target_z
    chosen = one_hot(jnp.logical_and(inside, lanes == target))
    near_high, rest = split(near)
    near_middle, near_low = split(rest)
    placed = matmul(
        jnp.concatenate([near_high, near_middle, near_low.astype(BF16)], axis=0), chosen
    )
    node_out[...] = placed[0:16] + placed[16:32] + placed[32:48]


def library_kernel(grid, count, coefficients, *refs):
    parts = [ref[...] for ref in refs[:count]]
    residual_out, gram_out, moment_out, terms = refs[count:]
    while len(parts) > 1:
        parts = [parts[k] + parts[k + 1] for k in range(0, len(parts), 2)]
    fields = parts[0]
    size_x, size_y, size_z = grid
    nodes = size_x * size_y * size_z
    lanes = lax.broadcasted_iota(jnp.int32, (1, nodes), 1)
    node_x = lanes // (size_y * size_z)
    node_y = (lanes // size_z) % size_y
    node_z = lanes % size_z
    rows = row_ids((8, nodes))
    density = fields[0:1]
    values = jnp.where(rows == 0, fields[0:8], fields[0:8] / (density + MASS_SHIFT))

    def moved(value, step):
        return pltpu.roll(value, step % nodes, 1)

    plane = size_y * size_z
    slope_x = (moved(values, -plane) - moved(values, plane)) * 0.5
    after_y = jnp.where(
        node_y == size_y - 1, moved(values, (size_y - 1) * size_z), moved(values, -size_z)
    )
    before_y = jnp.where(
        node_y == 0, moved(values, -(size_y - 1) * size_z), moved(values, size_z)
    )
    slope_y = (after_y - before_y) * 0.5
    after_z = jnp.where(node_z == size_z - 1, 0.0, moved(values, -1))
    before_z = jnp.where(node_z == 0, 0.0, moved(values, 1))
    slope_z = (after_z - before_z) * 0.5
    slopes = [[table[k : k + 1] for k in range(4)] for table in (slope_x, slope_y, slope_z)]
    strain = [
        [0.5 * (slopes[left][1 + right] + slopes[right][1 + left]) for right in range(3)]
        for left in range(3)
    ]
    divergence = strain[0][0] + strain[1][1] + strain[2][2]
    rate_sum = jnp.zeros_like(density)
    for left in range(3):
        for right in range(3):
            entry = strain[left][right]
            if left == right:
                entry = entry - divergence / 3.0
            rate_sum = rate_sum + entry * entry
    shear_rate = jnp.sqrt(2.0 * rate_sum + 0.01)
    stress = [fields[4 + k : 5 + k] for k in range(6)]
    pressure = (stress[0] + stress[3] + stress[5]) / 3.0
    deviator = (
        (stress[0] - pressure) ** 2
        + (stress[3] - pressure) ** 2
        + (stress[5] - pressure) ** 2
        + 2.0 * (stress[1] ** 2 + stress[2] ** 2 + stress[4] ** 2)
    )
    shear_stress = jnp.sqrt(0.5 * deviator + 0.01)
    pressure_scale = jnp.sqrt(pressure * pressure + 1.0)
    friction = shear_stress / pressure_scale
    features = [
        density,
        pressure / pressure_scale,
        shear_rate,
        shear_rate / jnp.sqrt(pressure_scale),
        divergence,
        slopes[0][0],
        slopes[1][0],
        slopes[2][0],
    ]
    entries = list(features)
    for left in range(8):
        for right in range(left, 8):
            entries.append(features[left] * features[right])
    for left in range(1, 5):
        entries.append(features[left] * features[left] * features[left])
    model = jnp.zeros_like(density)
    for k, entry in enumerate(entries):
        terms[k : k + 1, :] = entry
        model = model + coefficients[k] * entry
    residual = friction - model
    table = terms[...]
    gram_out[...] = (
        lax.dot_general(
            table,
            table,
            (((1,), (1,)), ((), ())),
            precision=lax.Precision.HIGHEST,
            preferred_element_type=F32,
        )
        / nodes
    )
    moment = lax.dot_general(
        jnp.broadcast_to(friction, (8, nodes)),
        table,
        (((1,), (1,)), ((), ())),
        precision=lax.Precision.HIGHEST,
        preferred_element_type=F32,
    )
    moment_out[...] = moment[0:1] / nodes
    down = lax.axis_index("down")
    cross = lax.axis_index("cross")
    depth = lax.axis_index("depth")
    b_rows = lax.broadcasted_iota(jnp.int32, (2, 1), 0)
    z_lanes = lax.broadcasted_iota(jnp.int32, (2, 2), 1)
    for a in range(2):
        mine = jnp.logical_and(node_x == down * 2 + a, node_y == cross * 2 + b_rows)
        column = [
            jnp.sum(
                jnp.where(jnp.logical_and(mine, node_z == depth * 2 + z), residual, 0.0),
                axis=1,
                keepdims=True,
            )
            for z in range(2)
        ]
        residual_out[a] = jnp.where(z_lanes == 0, column[0], column[1])


def ring(axis, step):
    peers = lax.axis_size(axis)
    return [(i, (i + step) % peers) for i in range(peers)]


def exchange(own, inner, height):
    cross = lax.axis_size("cross")

    def cells(block, first, count):
        return block[first * height : (first + count) * height]

    depth_halo = lax.ppermute(inner, "depth", [(0, 1), (1, 0)])
    if cross == 2:
        side = lax.ppermute(own, "cross", [(0, 1), (1, 0)])
        diag = lax.ppermute(inner, ("cross", "depth"), [(i, 3 - i) for i in range(4)])
        sides = [side, diag]

        def lateral(x):
            return [
                cells(side, x * 4 + 2, 2),
                cells(side, x * 4, 2),
                cells(diag, x * 2 + 1, 1),
                cells(diag, x * 2, 1),
            ]

    else:
        pairs = [(i * 2 + j, ((i + 1) % cross) * 2 + 1 - j) for i in range(cross) for j in range(2)]
        back = [(i * 2 + j, ((i - 1) % cross) * 2 + 1 - j) for i in range(cross) for j in range(2)]
        last = jnp.concatenate([cells(own, 2, 2), cells(own, 6, 2)], axis=0)
        first = jnp.concatenate([cells(own, 0, 2), cells(own, 4, 2)], axis=0)
        last_inner = jnp.concatenate([cells(inner, 1, 1), cells(inner, 3, 1)], axis=0)
        first_inner = jnp.concatenate([cells(inner, 0, 1), cells(inner, 2, 1)], axis=0)
        before = lax.ppermute(last, "cross", ring("cross", 1))
        after = lax.ppermute(first, "cross", ring("cross", -1))
        diag_before = lax.ppermute(last_inner, ("cross", "depth"), pairs)
        diag_after = lax.ppermute(first_inner, ("cross", "depth"), back)
        sides = [before, after, diag_before, diag_after]

        def lateral(x):
            return [
                cells(before, x * 2, 2),
                cells(after, x * 2, 2),
                cells(diag_before, x, 1),
                cells(diag_after, x, 1),
            ]

    def face(x):
        return jnp.concatenate([cells(own, x * 4, 4), cells(depth_halo, x * 2, 2)] + lateral(x), axis=0)

    x_before = lax.ppermute(face(1), "down", ring("down", 1))
    x_after = lax.ppermute(face(0), "down", ring("down", -1))
    return [own, depth_halo] + sides + [x_before, x_after]


def shared(value, axes, peers):
    return [value] + [
        lax.ppermute(value, axes, [(i, i ^ k) for i in range(peers)]) for k in range(1, peers)
    ]


def tree_sum(parts):
    while len(parts) > 1:
        parts = [parts[k] + parts[k + 1] for k in range(0, len(parts), 2)]
    return parts[0]


def body(positions, velocities, sphere_radii, counts, coefficients):
    down, cross, depth = (lax.axis_size(name) for name in ("down", "cross", "depth"))
    wide = cross != 2
    grid = (2 * down, 2 * cross, 2 * depth)
    nodes = grid[0] * grid[1] * grid[2]
    params = pltpu.CompilerParams(vmem_limit_bytes=VMEM_LIMIT)
    vector_shape = jax.ShapeDtypeStruct((3, 2, 2, 2, S), F32)

    def rows(count):
        return jax.ShapeDtypeStruct((count, S), F32)

    own, inner = pl.pallas_call(
        pack_kernel,
        out_shape=(rows(64), rows(32)),
        in_specs=[SMEM_SPEC] + [pl.BlockSpec(memory_space=pl.ANY)] * 3,
        out_specs=(VMEM_SPEC, VMEM_SPEC),
        scratch_shapes=[
            pltpu.VMEM((3, 2, 2, 2, S), F32),
            pltpu.VMEM((3, 2, 2, 2, S), F32),
            pltpu.VMEM((2, 2, 2, S), F32),
            pltpu.SemaphoreType.DMA((3,)),
        ],
        compiler_params=params,
        name="pack",
    )(counts, positions, velocities, sphere_radii)
    pieces = exchange(own, inner, 8)
    velocity_new, own_speed, inner_speed = pl.pallas_call(
        functools.partial(step_kernel, wide),
        out_shape=(vector_shape, rows(32), rows(16)),
        in_specs=[VMEM_SPEC] * len(pieces),
        out_specs=(VMEM_SPEC,) * 3,
        scratch_shapes=contact_scratch(3),
        compiler_params=params,
        name="step",
    )(*pieces)
    speeds = exchange(own_speed, inner_speed, 4)
    force_next, partial = pl.pallas_call(
        functools.partial(field_kernel, wide, grid),
        out_shape=(vector_shape, jax.ShapeDtypeStruct((16, nodes), F32)),
        in_specs=[VMEM_SPEC] * (len(pieces) + len(speeds)),
        out_specs=(VMEM_SPEC,) * 2,
        scratch_shapes=[pltpu.VMEM((16, 8 * S), F32)] + contact_scratch(9),
        compiler_params=params,
        name="field",
    )(*pieces, *speeds)
    partial = tree_sum(shared(partial, ("cross", "depth"), cross * depth))
    parts = shared(partial, "down", down)
    residual_field, gram_matrix, moment = pl.pallas_call(
        functools.partial(library_kernel, grid, len(parts)),
        out_shape=(
            jax.ShapeDtypeStruct((2, 2, 2), F32),
            jax.ShapeDtypeStruct((TERMS, TERMS), F32),
            jax.ShapeDtypeStruct((1, TERMS), F32),
        ),
        in_specs=[SMEM_SPEC] + [VMEM_SPEC] * len(parts),
        out_specs=(VMEM_SPEC,) * 3,
        scratch_shapes=[pltpu.VMEM((TERMS, nodes), F32)],
        compiler_params=params,
        name="library",
    )(coefficients, *parts)
    return (velocity_new, force_next, residual_field, gram_matrix, moment.reshape(TERMS))


def solution(mesh):
    return jax.shard_map(
        body,
        mesh=mesh,
        in_specs=(
            P(None, ("groups", "down"), "cross", "depth", None),
            P(None, ("groups", "down"), "cross", "depth", None),
            P(("groups", "down"), "cross", "depth", None),
            P(("groups", "down"), "cross", "depth"),
            P(),
        ),
        out_specs=(
            P(None, ("groups", "down"), "cross", "depth", None),
            P(None, ("groups", "down"), "cross", "depth", None),
            P(("groups", "down"), "cross", "depth"),
            P("groups", None),
            P("groups"),
        ),
        check_vma=False,
    )
```

profile of v0, /device:TPU:0, one launch (start us, length us, event | category | flops | bytes accessed | tf_op | source)
XLA Modules:
  0.0 57.8 jit_solution(7911150324621569472)
XLA Ops:
  0.6 0.7 %copy-done = f32[3,2,2,2,128]{4,3,2,1,0:T(2,128)S(1)} copy-done((f32[3,2,2,2,128]{4,3,2,1,0:T(2,128)S(1)}, f32[3,2,2,2,128]{4,3,2,1,0:T(2,128)}, u32[]{:S(2)}) %copy-start) | copy-done | bytes 12312
  1.3 0.7 %copy-done.1 = f32[3,2,2,2,128]{4,3,2,1,0:T(2,128)S(1)} copy-done((f32[3,2,2,2,128]{4,3,2,1,0:T(2,128)S(1)}, f32[3,2,2,2,128]{4,3,2,1,0:T(2,128)}, u32[]{:S(2)}) %copy-start.1) | copy-done | bytes 12312
  2.0 0.7 %copy-done.2 = f32[2,2,2,128]{3,2,1,0:T(2,128)S(1)} copy-done((f32[2,2,2,128]{3,2,1,0:T(2,128)S(1)}, f32[2,2,2,128]{3,2,1,0:T(2,128)}, u32[]{:S(2)}) %copy-start.2) | copy-done | bytes 4120
  2.7 0.7 %copy-done.3 = s32[2,2,2]{2,1,0:T(2,128)S(1)} copy-done((s32[2,2,2]{2,1,0:T(2,128)S(1)}, s32[2,2,2]{2,1,0:T(2,128)}, u32[]{:S(2)}) %copy-start.3) | copy-done | bytes 56
  3.4 0.7 %pack.1 = (f32[64,128]{1,0:T(8,128)S(1)}, f32[32,128]{1,0:T(8,128)S(1)}) custom-call(s32[2,2,2]{2,1,0:T(2,128)S(1)} %copy-done.3, f32[3,2,2,2,128]{4,3,2,1,0:T(2,128)S(1)} %copy-done, f32[3,2,2,2,128]{4,3,2,1,0:T(2,128)S(1)} %copy-done.1, f32[2,2,2,128]{3,2,1,0:T(2,128)S(1)} %copy-done.2), custom_call_target="tpu_custom_call" | custom-call | tf_op jit(solution)/shard_map/pack/pallas_call | solution.py:558
  4.1 2.4 %collective-permute-start.2 = (f32[32,128]{1,0:T(8,128)S(1)}, f32[32,128]{1,0:T(8,128)S(1)}, u32[]{:S(2)}, u32[]{:S(2)}) collective-permute-start(f32[32,128]{1,0:T(8,128)S(1)} %get-tuple-element.16), channel_id=1, source_target_pairs={{0,3},{1,2},{2,1},{3,0},{4,7},{5,6},{6,5},{7,4},{8,11},{9,10},{10,... | collective-permute-start | bytes 49160 | tf_op jit(solution)/shard_map/ppermute | solution.py:495
  6.5 0.7 %collective-permute-start = (f32[32,128]{1,0:T(8,128)S(1)}, f32[32,128]{1,0:T(8,128)S(1)}, u32[]{:S(2)}, u32[]{:S(2)}) collective-permute-start(f32[32,128]{1,0:T(8,128)S(1)} %get-tuple-element.16), channel_id=1, source_target_pairs={{0,1},{1,0},{2,3},{3,2},{4,5},{5,4},{6,7},{7,6},{8,9},{9,8},{10,11... | collective-permute-start | bytes 49160 | tf_op jit(solution)/shard_map/ppermute | solution.py:492
  7.2 0.0 collective-permute-start.1
  7.3 0.8 %collective-permute-done.refs_1_ = f32[32,128]{1,0:T(8,128)S(1)} collective-permute-done((f32[32,128]{1,0:T(8,128)S(1)}, f32[32,128]{1,0:T(8,128)S(1)}, u32[]{:S(2)}, u32[]{:S(2)}) %collective-permute-start) | collective-permute-done | bytes 16416 | tf_op jit(solution)/shard_map/ppermute | solution.py:492
  8.1 3.1 %collective-permute-done.1.refs_2_ = f32[64,128]{1,0:T(8,128)S(1)} collective-permute-done((f32[64,128]{1,0:T(8,128)S(1)}, f32[64,128]{1,0:T(8,128)S(1)}, u32[]{:S(2)}, u32[]{:S(2)}) %collective-permute-start.1) | collective-permute-done | bytes 32800 | tf_op jit(solution)/shard_map/ppermute | solution.py:494
  11.2 3.7 %collective-permute-start.4 = (f32[96,128]{1,0:T(8,128)S(1)}, f32[96,128]{1,0:T(8,128)S(1)}, u32[]{:S(2)}, u32[]{:S(2)}) collective-permute-start(f32[96,128]{1,0:T(8,128)S(1)} %get-tuple-element.37), channel_id=1, source_target_pairs={{0,12},{4,0},{8,4},{12,8},{1,13},{5,1},{9,5},{13,9},{2,14},{6,2},{... | collective-permute-start | bytes 147464 | tf_op jit(solution)/shard_map/ppermute | solution.py:531
  14.8 0.0 collective-permute-start.3
  14.8 1.7 %collective-permute-done.4.refs_5_ = f32[96,128]{1,0:T(8,128)S(1)} collective-permute-done((f32[96,128]{1,0:T(8,128)S(1)}, f32[96,128]{1,0:T(8,128)S(1)}, u32[]{:S(2)}, u32[]{:S(2)}) %collective-permute-start.4) | collective-permute-done | bytes 49184 | tf_op jit(solution)/shard_map/ppermute | solution.py:531
  16.6 4.1 %collective-permute-done.3.refs_4_ = f32[96,128]{1,0:T(8,128)S(1)} collective-permute-done((f32[96,128]{1,0:T(8,128)S(1)}, f32[96,128]{1,0:T(8,128)S(1)}, u32[]{:S(2)}, u32[]{:S(2)}) %collective-permute-start.3) | collective-permute-done | bytes 49184 | tf_op jit(solution)/shard_map/ppermute | solution.py:530
  20.7 6.0 %step.1 = (f32[3,2,2,2,128]{4,3,2,1,0:T(2,128)}, f32[32,128]{1,0:T(8,128)S(1)}, f32[16,128]{1,0:T(8,128)S(1)}) custom-call(f32[64,128]{1,0:T(8,128)S(1)} %get-tuple-element.15.refs_0_, f32[32,128]{1,0:T(8,128)S(1)} %collective-permute-done.refs_1_, f32[64,128]{1,0:T(8,128)S(1)} %collective-permute-done.1.refs_2_, ...), custom_call_target="tpu_custom_call" | custom-call | tf_op jit(solution)/shard_map/step/pallas_call | solution.py:573
  26.7 0.5 collective-permute-start.5
  27.2 1.6 %collective-permute-start.6 = (f32[32,128]{1,0:T(8,128)S(1)}, f32[32,128]{1,0:T(8,128)S(1)}, u32[]{:S(2)}, u32[]{:S(2)}) collective-permute-start(f32[32,128]{1,0:T(8,128)S(1)} %get-tuple-element.18.refs_6_), channel_id=1, source_target_pairs={{0,2},{2,0},{1,3},{3,1},{4,6},{6,4},{5,7},{7,5},{8,10},{10,8},{9,1... | collective-permute-start | bytes 49160 | tf_op jit(solution)/shard_map/ppermute | solution.py:494
  28.9 0.9 %collective-permute-done.7.refs_9_ = f32[16,128]{1,0:T(8,128)S(1)} collective-permute-done((f32[16,128]{1,0:T(8,128)S(1)}, f32[16,128]{1,0:T(8,128)S(1)}, u32[]{:S(2)}, u32[]{:S(2)}) %collective-permute-start.7) | collective-permute-done | bytes 8224 | tf_op jit(solution)/shard_map/ppermute | solution.py:495
  29.8 1.1 %collective-permute-done.6.refs_8_ = f32[32,128]{1,0:T(8,128)S(1)} collective-permute-done((f32[32,128]{1,0:T(8,128)S(1)}, f32[32,128]{1,0:T(8,128)S(1)}, u32[]{:S(2)}, u32[]{:S(2)}) %collective-permute-start.6) | collective-permute-done | bytes 16416 | tf_op jit(solution)/shard_map/ppermute | solution.py:494
  31.0 0.0 collective-permute-start.8
  31.1 3.8 %collective-permute-start.9 = (f32[48,128]{1,0:T(8,128)S(1)}, f32[48,128]{1,0:T(8,128)S(1)}, u32[]{:S(2)}, u32[]{:S(2)}) collective-permute-start(f32[48,128]{1,0:T(8,128)S(1)} %concatenate.15), channel_id=1, source_target_pairs={{0,12},{4,0},{8,4},{12,8},{1,13},{5,1},{9,5},{13,9},{2,14},{6,2},{... | collective-permute-start | bytes 73736 | tf_op jit(solution)/shard_map/ppermute | solution.py:531
  34.9 1.7 %collective-permute-done.8.refs_10_ = f32[48,128]{1,0:T(8,128)S(1)} collective-permute-done((f32[48,128]{1,0:T(8,128)S(1)}, f32[48,128]{1,0:T(8,128)S(1)}, u32[]{:S(2)}, u32[]{:S(2)}) %collective-permute-start.8) | collective-permute-done | bytes 24608 | tf_op jit(solution)/shard_map/ppermute | solution.py:530
  36.6 7.4 %field.1 = (f32[3,2,2,2,128]{4,3,2,1,0:T(2,128)}, f32[16,128]{1,0:T(8,128)S(1)}) custom-call(f32[64,128]{1,0:T(8,128)S(1)} %get-tuple-element.15.refs_0_, f32[32,128]{1,0:T(8,128)S(1)} %collective-permute-done.refs_1_, f32[64,128]{1,0:T(8,128)S(1)} %collective-permute-done.1.refs_2_, f32[32,128]{1,0:T(8,128)S(1)} %collective-permute-done.2.refs_3_, ...), custom_call_target="tpu_custom_call" | custom-call | tf_op jit(solution)/shard_map/field/pallas_call | solution.py:583
  44.1 1.5 %collective-permute-start.11 = (f32[16,128]{1,0:T(8,128)S(1)}, f32[16,128]{1,0:T(8,128)S(1)}, u32[]{:S(2)}, u32[]{:S(2)}) collective-permute-start(f32[16,128]{1,0:T(8,128)S(1)} %get-tuple-element.21), channel_id=1, source_target_pairs={{0,2},{1,3},{2,0},{3,1},{4,6},{5,7},{6,4},{7,5},{8,10},{9,11},{10,... | collective-permute-start | bytes 24584 | tf_op jit(solution)/shard_map/ppermute | solution.py:537
  45.5 0.4 collective-permute-start.10
  45.9 1.3 %collective-permute-done.12 = f32[16,128]{1,0:T(8,128)S(1)} collective-permute-done((f32[16,128]{1,0:T(8,128)S(1)}, f32[16,128]{1,0:T(8,128)S(1)}, u32[]{:S(2)}, u32[]{:S(2)}) %collective-permute-start.12) | collective-permute-done | bytes 8224 | tf_op jit(solution)/shard_map/ppermute | solution.py:537
  47.2 0.5 collective-permute-done.11
  47.8 4.0 %collective-permute-start.15 = (f32[16,128]{1,0:T(8,128)S(1)}, f32[16,128]{1,0:T(8,128)S(1)}, u32[]{:S(2)}, u32[]{:S(2)}) collective-permute-start(f32[16,128]{1,0:T(8,128)S(1)} %add_add_fusion.refs_0_), channel_id=1, source_target_pairs={{0,12},{4,8},{8,4},{12,0},{1,13},{5,9},{9,5},{13,1},{2,14},{6,10},... | collective-permute-start | bytes 24584 | tf_op jit(solution)/shard_map/ppermute | solution.py:537
  51.7 0.6 %collective-permute-start.13 = (f32[16,128]{1,0:T(8,128)S(1)}, f32[16,128]{1,0:T(8,128)S(1)}, u32[]{:S(2)}, u32[]{:S(2)}) collective-permute-start(f32[16,128]{1,0:T(8,128)S(1)} %add_add_fusion.refs_0_), channel_id=1, source_target_pairs={{0,4},{4,0},{8,12},{12,8},{1,5},{5,1},{9,13},{13,9},{2,6},{6,2},{1... | collective-permute-start | bytes 24584 | tf_op jit(solution)/shard_map/ppermute | solution.py:537
  52.4 1.0 %collective-permute-done.15.refs_3_ = f32[16,128]{1,0:T(8,128)S(1)} collective-permute-done((f32[16,128]{1,0:T(8,128)S(1)}, f32[16,128]{1,0:T(8,128)S(1)}, u32[]{:S(2)}, u32[]{:S(2)}) %collective-permute-start.15) | collective-permute-done | bytes 8224 | tf_op jit(solution)/shard_map/ppermute | solution.py:537
  53.3 2.9 %collective-permute-done.14.refs_2_ = f32[16,128]{1,0:T(8,128)S(1)} collective-permute-done((f32[16,128]{1,0:T(8,128)S(1)}, f32[16,128]{1,0:T(8,128)S(1)}, u32[]{:S(2)}, u32[]{:S(2)}) %collective-permute-start.14) | collective-permute-done | bytes 8224 | tf_op jit(solution)/shard_map/ppermute | solution.py:537
  56.3 1.5 %library.1 = (f32[2,2,2]{2,1,0:T(2,128)}, f32[48,48]{1,0:T(8,128)}, f32[1,48]{1,0:T(1,128)}) custom-call(f32[48]{0:T(128)S(1)} %copy-done.4, f32[16,128]{1,0:T(8,128)S(1)} %add_add_fusion.refs_0_, f32[16,128]{1,0:T(8,128)S(1)} %collective-permute-done.13.refs_1_, f32[16,128]{1,0:T(8,128)S(1)} %collective-permute-done.14.refs_2_, ...), custom_call_target="tpu_custom_call" | custom-call | tf_op jit(solution)/shard_map/library/pallas_call | solution.py:594
  (27 shorter events, 0.1 us)
Async XLA Ops:
  0.6 0.7 %copy-start = (f32[3,2,2,2,128]{4,3,2,1,0:T(2,128)S(1)}, f32[3,2,2,2,128]{4,3,2,1,0:T(2,128)}, u32[]{:S(2)}) copy-start(f32[3,2,2,2,128]{4,3,2,1,0:T(2,128)} %positions_hbm.1) | copy-start | bytes 36868
  1.3 0.7 %copy-start.1 = (f32[3,2,2,2,128]{4,3,2,1,0:T(2,128)S(1)}, f32[3,2,2,2,128]{4,3,2,1,0:T(2,128)}, u32[]{:S(2)}) copy-start(f32[3,2,2,2,128]{4,3,2,1,0:T(2,128)} %velocities_hbm.1) | copy-start | bytes 36868
  2.0 0.7 %copy-start.2 = (f32[2,2,2,128]{3,2,1,0:T(2,128)S(1)}, f32[2,2,2,128]{3,2,1,0:T(2,128)}, u32[]{:S(2)}) copy-start(f32[2,2,2,128]{3,2,1,0:T(2,128)} %radii_hbm.1) | copy-start | bytes 12292
  2.7 0.7 %copy-start.3 = (s32[2,2,2]{2,1,0:T(2,128)S(1)}, s32[2,2,2]{2,1,0:T(2,128)}, u32[]{:S(2)}) copy-start(s32[2,2,2]{2,1,0:T(2,128)} %counts.1) | copy-start | bytes 100
  4.1 7.0 %collective-permute-start.2 = (f32[32,128]{1,0:T(8,128)S(1)}, f32[32,128]{1,0:T(8,128)S(1)}, u32[]{:S(2)}, u32[]{:S(2)}) collective-permute-start(f32[32,128]{1,0:T(8,128)S(1)} %get-tuple-element.16), channel_id=1, source_target_pairs={{0,3},{1,2},{2,1},{3,0},{4,7},{5,6},{6,5},{7,4},{8,11},{9,10},{10,... | collective-permute-start | bytes 49160 | tf_op jit(solution)/shard_map/ppermute | solution.py:495
  6.5 1.5 %collective-permute-start = (f32[32,128]{1,0:T(8,128)S(1)}, f32[32,128]{1,0:T(8,128)S(1)}, u32[]{:S(2)}, u32[]{:S(2)}) collective-permute-start(f32[32,128]{1,0:T(8,128)S(1)} %get-tuple-element.16), channel_id=1, source_target_pairs={{0,1},{1,0},{2,3},{3,2},{4,5},{5,4},{6,7},{7,6},{8,9},{9,8},{10,11... | collective-permute-start | bytes 49160 | tf_op jit(solution)/shard_map/ppermute | solution.py:492
  7.2 3.9 %collective-permute-start.1 = (f32[64,128]{1,0:T(8,128)S(1)}, f32[64,128]{1,0:T(8,128)S(1)}, u32[]{:S(2)}, u32[]{:S(2)}) collective-permute-start(f32[64,128]{1,0:T(8,128)S(1)} %get-tuple-element.15.refs_0_), channel_id=1, source_target_pairs={{0,2},{2,0},{1,3},{3,1},{4,6},{6,4},{5,7},{7,5},{8,10},{10,8},{9,1... | collective-permute-start | bytes 98312 | tf_op jit(solution)/shard_map/ppermute | solution.py:494
  11.2 5.4 %collective-permute-start.4 = (f32[96,128]{1,0:T(8,128)S(1)}, f32[96,128]{1,0:T(8,128)S(1)}, u32[]{:S(2)}, u32[]{:S(2)}) collective-permute-start(f32[96,128]{1,0:T(8,128)S(1)} %get-tuple-element.37), channel_id=1, source_target_pairs={{0,12},{4,0},{8,4},{12,8},{1,13},{5,1},{9,5},{13,9},{2,14},{6,2},{... | collective-permute-start | bytes 147464 | tf_op jit(solution)/shard_map/ppermute | solution.py:531
  14.8 5.9 %collective-permute-start.3 = (f32[96,128]{1,0:T(8,128)S(1)}, f32[96,128]{1,0:T(8,128)S(1)}, u32[]{:S(2)}, u32[]{:S(2)}) collective-permute-start(f32[96,128]{1,0:T(8,128)S(1)} %get-tuple-element.38), channel_id=1, source_target_pairs={{0,4},{4,8},{8,12},{12,0},{1,5},{5,9},{9,13},{13,1},{2,6},{6,10},{... | collective-permute-start | bytes 147464 | tf_op jit(solution)/shard_map/ppermute | solution.py:530
  26.7 3.1 %collective-permute-start.7 = (f32[16,128]{1,0:T(8,128)S(1)}, f32[16,128]{1,0:T(8,128)S(1)}, u32[]{:S(2)}, u32[]{:S(2)}) collective-permute-start(f32[16,128]{1,0:T(8,128)S(1)} %get-tuple-element.19), channel_id=1, source_target_pairs={{0,3},{1,2},{2,1},{3,0},{4,7},{5,6},{6,5},{7,4},{8,11},{9,10},{10,... | collective-permute-start | bytes 24584 | tf_op jit(solution)/shard_map/ppermute | solution.py:495
  26.7 3.1 %collective-permute-start.5 = (f32[16,128]{1,0:T(8,128)S(1)}, f32[16,128]{1,0:T(8,128)S(1)}, u32[]{:S(2)}, u32[]{:S(2)}) collective-permute-start(f32[16,128]{1,0:T(8,128)S(1)} %get-tuple-element.19), channel_id=1, source_target_pairs={{0,1},{1,0},{2,3},{3,2},{4,5},{5,4},{6,7},{7,6},{8,9},{9,8},{10,11... | collective-permute-start | bytes 24584 | tf_op jit(solution)/shard_map/ppermute | solution.py:492
  27.2 3.7 %collective-permute-start.6 = (f32[32,128]{1,0:T(8,128)S(1)}, f32[32,128]{1,0:T(8,128)S(1)}, u32[]{:S(2)}, u32[]{:S(2)}) collective-permute-start(f32[32,128]{1,0:T(8,128)S(1)} %get-tuple-element.18.refs_6_), channel_id=1, source_target_pairs={{0,2},{2,0},{1,3},{3,1},{4,6},{6,4},{5,7},{7,5},{8,10},{10,8},{9,1... | collective-permute-start | bytes 49160 | tf_op jit(solution)/shard_map/ppermute | solution.py:494
  31.0 5.7 %collective-permute-start.8 = (f32[48,128]{1,0:T(8,128)S(1)}, f32[48,128]{1,0:T(8,128)S(1)}, u32[]{:S(2)}, u32[]{:S(2)}) collective-permute-start(f32[48,128]{1,0:T(8,128)S(1)} %concatenate.14), channel_id=1, source_target_pairs={{0,4},{4,8},{8,12},{12,0},{1,5},{5,9},{9,13},{13,1},{2,6},{6,10},{... | collective-permute-start | bytes 73736 | tf_op jit(solution)/shard_map/ppermute | solution.py:530
  31.1 5.6 %collective-permute-start.9 = (f32[48,128]{1,0:T(8,128)S(1)}, f32[48,128]{1,0:T(8,128)S(1)}, u32[]{:S(2)}, u32[]{:S(2)}) collective-permute-start(f32[48,128]{1,0:T(8,128)S(1)} %concatenate.15), channel_id=1, source_target_pairs={{0,12},{4,0},{8,4},{12,8},{1,13},{5,1},{9,5},{13,9},{2,14},{6,2},{... | collective-permute-start | bytes 73736 | tf_op jit(solution)/shard_map/ppermute | solution.py:531
  44.1 12.2 %copy-start.4 = (f32[48]{0:T(128)S(1)}, f32[48]{0:T(128)}, u32[]{:S(2)}) copy-start(f32[48]{0:T(128)} %coefficients.1) | copy-start | bytes 580
  44.1 3.1 %collective-permute-start.12 = (f32[16,128]{1,0:T(8,128)S(1)}, f32[16,128]{1,0:T(8,128)S(1)}, u32[]{:S(2)}, u32[]{:S(2)}) collective-permute-start(f32[16,128]{1,0:T(8,128)S(1)} %get-tuple-element.21), channel_id=1, source_target_pairs={{0,3},{1,2},{2,1},{3,0},{4,7},{5,6},{6,5},{7,4},{8,11},{9,10},{10,... | collective-permute-start | bytes 24584 | tf_op jit(solution)/shard_map/ppermute | solution.py:537
  44.1 3.7 %collective-permute-start.11 = (f32[16,128]{1,0:T(8,128)S(1)}, f32[16,128]{1,0:T(8,128)S(1)}, u32[]{:S(2)}, u32[]{:S(2)}) collective-permute-start(f32[16,128]{1,0:T(8,128)S(1)} %get-tuple-element.21), channel_id=1, source_target_pairs={{0,2},{1,3},{2,0},{3,1},{4,6},{5,7},{6,4},{7,5},{8,10},{9,11},{10,... | collective-permute-start | bytes 24584 | tf_op jit(solution)/shard_map/ppermute | solution.py:537
  45.5 2.2 %collective-permute-start.10 = (f32[16,128]{1,0:T(8,128)S(1)}, f32[16,128]{1,0:T(8,128)S(1)}, u32[]{:S(2)}, u32[]{:S(2)}) collective-permute-start(f32[16,128]{1,0:T(8,128)S(1)} %get-tuple-element.21), channel_id=1, source_target_pairs={{0,1},{1,0},{2,3},{3,2},{4,5},{5,4},{6,7},{7,6},{8,9},{9,8},{10,11... | collective-permute-start | bytes 24584 | tf_op jit(solution)/shard_map/ppermute | solution.py:537
  47.8 5.6 %collective-permute-start.15 = (f32[16,128]{1,0:T(8,128)S(1)}, f32[16,128]{1,0:T(8,128)S(1)}, u32[]{:S(2)}, u32[]{:S(2)}) collective-permute-start(f32[16,128]{1,0:T(8,128)S(1)} %add_add_fusion.refs_0_), channel_id=1, source_target_pairs={{0,12},{4,8},{8,4},{12,0},{1,13},{5,9},{9,5},{13,1},{2,14},{6,10},... | collective-permute-start | bytes 24584 | tf_op jit(solution)/shard_map/ppermute | solution.py:537
  51.7 4.5 %collective-permute-start.14 = (f32[16,128]{1,0:T(8,128)S(1)}, f32[16,128]{1,0:T(8,128)S(1)}, u32[]{:S(2)}, u32[]{:S(2)}) collective-permute-start(f32[16,128]{1,0:T(8,128)S(1)} %add_add_fusion.refs_0_), channel_id=1, source_target_pairs={{0,8},{4,12},{8,0},{12,4},{1,9},{5,13},{9,1},{13,5},{2,10},{6,14},... | collective-permute-start | bytes 24584 | tf_op jit(solution)/shard_map/ppermute | solution.py:537
  51.7 4.5 %collective-permute-start.13 = (f32[16,128]{1,0:T(8,128)S(1)}, f32[16,128]{1,0:T(8,128)S(1)}, u32[]{:S(2)}, u32[]{:S(2)}) collective-permute-start(f32[16,128]{1,0:T(8,128)S(1)} %add_add_fusion.refs_0_), channel_id=1, source_target_pairs={{0,4},{4,0},{8,12},{12,8},{1,5},{5,1},{9,13},{13,9},{2,6},{6,2},{1... | collective-permute-start | bytes 24584 | tf_op jit(solution)/shard_map/ppermute | solution.py:537
where the time goes:
time: 58.1 us; the launch traced here: 57.8 us
  starting transfers between devices  19.3 us (33%)
  waiting for transfers between devices  19.3 us (33%)
  Pallas kernels  15.6 us (27%)
  local copies, waits for them, and re-layouts  2.86 us (5%)
  between operations  0.71 us (1%)
    ppermute x2, starting transfers between devices, exchange(): x_after = lax.ppermute(face(0), 'down', ring('down', -1))  7.5 us
    pallas_call x1, Pallas kernels, body(): pl.pallas_call(functools.partial(field_kernel, wide, grid), out_shape=(ve...  7.41 us
    ppermute x6, starting transfers between devices, shared(): lax.ppermute(value, axes, [(i, i ^ k) for i in range(peers)])  6.47 us
    pallas_call x1, Pallas kernels, body(): pl.pallas_call(functools.partial(step_kernel, wide), out_shape=(vector_sh...  6.01 us
    ppermute x2, waiting for transfers between devices, exchange(): x_before = lax.ppermute(face(1), 'down', ring('down', 1))  5.87 us
    ppermute x6, waiting for transfers between devices, shared(): lax.ppermute(value, axes, [(i, i ^ k) for i in range(peers)])  5.73 us
    ppermute x2, waiting for transfers between devices, exchange(): side = lax.ppermute(own, 'cross', [(0, 1), (1, 0)])  4.22 us
    unnamed x15, local copies, waits for them, and re-layouts  2.79 us
  transfers between devices with their start and end apart: 16, of which 11 were waited for; matrix products, arithmetic and copies ran while one was open for 0% of the time, Pallas kernels for 0%

commit v1 on v0

--- a/solution.py
+++ b/solution.py
@@ -364,12 +364,8 @@
     node_out[...] = placed[0:16] + placed[16:32] + placed[32:48]
 
 
-def library_kernel(grid, count, coefficients, *refs):
-    parts = [ref[...] for ref in refs[:count]]
-    residual_out, gram_out, moment_out, terms = refs[count:]
-    while len(parts) > 1:
-        parts = [parts[k] + parts[k + 1] for k in range(0, len(parts), 2)]
-    fields = parts[0]
+def library_kernel(grid, coefficients, parts, residual_out, gram_out, moment_out, terms):
+    fields = jnp.sum(parts[...], axis=0)
     size_x, size_y, size_z = grid
     nodes = size_x * size_y * size_z
     lanes = lax.broadcasted_iota(jnp.int32, (1, nodes), 1)
@@ -532,18 +528,6 @@
     return [own, depth_halo] + sides + [x_before, x_after]
 
 
-def shared(value, axes, peers):
-    return [value] + [
-        lax.ppermute(value, axes, [(i, i ^ k) for i in range(peers)]) for k in range(1, peers)
-    ]
-
-
-def tree_sum(parts):
-    while len(parts) > 1:
-        parts = [parts[k] + parts[k + 1] for k in range(0, len(parts), 2)]
-    return parts[0]
-
-
 def body(positions, velocities, sphere_radii, counts, coefficients):
     down, cross, depth = (lax.axis_size(name) for name in ("down", "cross", "depth"))
     wide = cross != 2
@@ -566,7 +550,7 @@
             pltpu.VMEM((2, 2, 2, S), F32),
             pltpu.SemaphoreType.DMA((3,)),
         ],
-        compiler_params=params,
+        compiler_params=pltpu.CompilerParams(vmem_limit_bytes=60 * 1024 * 1024),
         name="pack",
     )(counts, positions, velocities, sphere_radii)
     pieces = exchange(own, inner, 8)
@@ -589,21 +573,23 @@
         compiler_params=params,
         name="field",
     )(*pieces, *speeds)
-    partial = tree_sum(shared(partial, ("cross", "depth"), cross * depth))
-    parts = shared(partial, "down", down)
+    peers = down * cross * depth
+    parts = lax.all_to_all(
+        jnp.broadcast_to(partial, (peers, 16, nodes)), ("down", "cross", "depth"), 0, 0
+    )
     residual_field, gram_matrix, moment = pl.pallas_call(
-        functools.partial(library_kernel, grid, len(parts)),
+        functools.partial(library_kernel, grid),
         out_shape=(
             jax.ShapeDtypeStruct((2, 2, 2), F32),
             jax.ShapeDtypeStruct((TERMS, TERMS), F32),
             jax.ShapeDtypeStruct((1, TERMS), F32),
         ),
-        in_specs=[SMEM_SPEC] + [VMEM_SPEC] * len(parts),
+        in_specs=[SMEM_SPEC, VMEM_SPEC],
         out_specs=(VMEM_SPEC,) * 3,
         scratch_shapes=[pltpu.VMEM((TERMS, nodes), F32)],
         compiler_params=params,
         name="library",
-    )(coefficients, *parts)
+    )(coefficients, parts)
     return (velocity_new, force_next, residual_field, gram_matrix, moment.reshape(TERMS))
 
 

time: 58.1 us -> 60.4 us (1.040)
  blocking collectives: 0 us -> 14.2 us
  starting transfers between devices: 19.3 us -> 12.9 us
  waiting for transfers between devices: 19.3 us -> 13.2 us
  Pallas kernels: 15.6 us -> 18.2 us
  local copies, waits for them, and re-layouts: 2.86 us -> 0.85 us
    all_to_all x0 -> x1, blocking collectives: none -> 14.2 us  [body(): lax.all_to_all(jnp.broadcast_to(partial, (peers, 16, nodes)), ('down', 'c...]
    ppermute x6 -> x0, starting transfers between devices: 6.47 us -> none  [shared(): lax.ppermute(value, axes, [(i, i ^ k) for i in range(peers)])]
    ppermute x6 -> x0, waiting for transfers between devices: 5.73 us -> none  [shared(): lax.ppermute(value, axes, [(i, i ^ k) for i in range(peers)])]
    unnamed x15 -> x9, local copies, waits for them, and re-layouts: 2.79 us -> 0.77 us
    pallas_call x1, Pallas kernels: 0.67 us -> 2.08 us  [body(): pl.pallas_call(pack_kernel, out_shape=(rows(64), rows(32)), in_specs=[SME...]
    pallas_call x1, Pallas kernels: 7.41 us -> 8.46 us  [body(): pl.pallas_call(functools.partial(field_kernel, wide, grid), out_shape=(ve...]
  transfers between devices with their start and end apart: 16 -> 10, of which waited for: 11 -> 7; matrix products, arithmetic and copies ran while one was open for 0% -> 1% of each run, Pallas kernels for 0% -> 0%
where the time goes in v1:
time: 60.4 us; the launch traced here: 59.9 us
  Pallas kernels  18.2 us (30%)
  blocking collectives  14.2 us (24%)
  waiting for transfers between devices  13.2 us (22%)
  starting transfers between devices  12.9 us (21%)
  local copies, waits for them, and re-layouts  0.85 us (1%)
  between operations  0.7 us (1%)
    all_to_all x1, blocking collectives, body(): lax.all_to_all(jnp.broadcast_to(partial, (peers, 16, nodes)), ('down', 'c...  14.2 us
    pallas_call x1, Pallas kernels, body(): pl.pallas_call(functools.partial(field_kernel, wide, grid), out_shape=(ve...  8.46 us
    ppermute x2, starting transfers between devices, exchange(): x_after = lax.ppermute(face(0), 'down', ring('down', -1))  7.5 us
    pallas_call x1, Pallas kernels, body(): pl.pallas_call(functools.partial(step_kernel, wide), out_shape=(vector_sh...  6.16 us
    ppermute x2, waiting for transfers between devices, exchange(): x_before = lax.ppermute(face(1), 'down', ring('down', 1))  5.87 us
    ppermute x2, waiting for transfers between devices, exchange(): side = lax.ppermute(own, 'cross', [(0, 1), (1, 0)])  4.37 us
    ppermute x2, starting transfers between devices, exchange(): lax.ppermute(inner, ('cross', 'depth'), [(i, 3 - i) for i in range(4)])  2.45 us
    pallas_call x1, Pallas kernels, body(): pl.pallas_call(pack_kernel, out_shape=(rows(64), rows(32)), in_specs=[SME...  2.08 us
  transfers between devices with their start and end apart: 10, of which 7 were waited for; matrix products, arithmetic and copies ran while one was open for 1% of the time, Pallas kernels for 0%

profile of v1, /device:TPU:0, one launch (start us, length us, event | category | flops | bytes accessed | tf_op | source)
XLA Modules:
  0.0 59.9 jit_solution(17049405687931404880)
XLA Ops:
  0.6 2.1 %pack.1 = (f32[64,128]{1,0:T(8,128)}, f32[32,128]{1,0:T(8,128)}) custom-call(s32[2,2,2]{2,1,0:T(2,128)} %counts.1, f32[3,2,2,2,128]{4,3,2,1,0:T(2,128)} %positions_hbm.1, f32[3,2,2,2,128]{4,3,2,1,0:T(2,128)} %velocities_hbm.1, f32[2,2,2,128]{3,2,1,0:T(2,128)} %radii_hbm.1), custom_call_target="tpu_custom_call" | custom-call | tf_op jit(solution)/shard_map/pack/pallas_call | solution.py:542
  2.7 2.4 %collective-permute-start.2 = (f32[32,128]{1,0:T(8,128)}, f32[32,128]{1,0:T(8,128)S(1)}, u32[]{:S(2)}, u32[]{:S(2)}) collective-permute-start(f32[32,128]{1,0:T(8,128)} %get-tuple-element.16), channel_id=1, source_target_pairs={{0,3},{1,2},{2,1},{3,0},{4,7},{5,6},{6,5},{7,4},{8,11},{9,10},{10,... | collective-permute-start | bytes 49160 | tf_op jit(solution)/shard_map/ppermute | solution.py:491
  5.2 0.7 %collective-permute-start = (f32[32,128]{1,0:T(8,128)}, f32[32,128]{1,0:T(8,128)S(1)}, u32[]{:S(2)}, u32[]{:S(2)}) collective-permute-start(f32[32,128]{1,0:T(8,128)} %get-tuple-element.16), channel_id=1, source_target_pairs={{0,1},{1,0},{2,3},{3,2},{4,5},{5,4},{6,7},{7,6},{8,9},{9,8},{10,11... | collective-permute-start | bytes 49160 | tf_op jit(solution)/shard_map/ppermute | solution.py:488
  5.8 0.0 collective-permute-start.1
  5.9 0.8 %constant_dynamic-update-slice_fusion.11 = (f32[96,128]{1,0:T(8,128)S(1)}, f32[96,128]{1,0:T(8,128)S(1)}) fusion(f32[64,128]{1,0:T(8,128)} %get-tuple-element.15.refs_0_), kind=kLoop, calls=%fused_computation.11 | loop fusion | bytes 65536
  6.6 0.3 collective-permute-done.refs_1_
  6.9 3.1 %collective-permute-done.1.refs_2_ = f32[64,128]{1,0:T(8,128)S(1)} collective-permute-done((f32[64,128]{1,0:T(8,128)}, f32[64,128]{1,0:T(8,128)S(1)}, u32[]{:S(2)}, u32[]{:S(2)}) %collective-permute-start.1) | collective-permute-done | bytes 32800 | tf_op jit(solution)/shard_map/ppermute | solution.py:490
  10.0 0.0 copy-start
  10.0 0.0 collective-permute-done.2.refs_3_
  10.0 3.7 %collective-permute-start.4 = (f32[96,128]{1,0:T(8,128)S(1)}, f32[96,128]{1,0:T(8,128)S(1)}, u32[]{:S(2)}, u32[]{:S(2)}) collective-permute-start(f32[96,128]{1,0:T(8,128)S(1)} %get-tuple-element.37), channel_id=1, source_target_pairs={{0,12},{4,0},{8,4},{12,8},{1,13},{5,1},{9,5},{13,9},{2,14},{6,2},{... | collective-permute-start | bytes 147464 | tf_op jit(solution)/shard_map/ppermute | solution.py:527
  13.7 0.0 collective-permute-start.3
  13.7 1.7 %collective-permute-done.4.refs_5_ = f32[96,128]{1,0:T(8,128)S(1)} collective-permute-done((f32[96,128]{1,0:T(8,128)S(1)}, f32[96,128]{1,0:T(8,128)S(1)}, u32[]{:S(2)}, u32[]{:S(2)}) %collective-permute-start.4) | collective-permute-done | bytes 49184 | tf_op jit(solution)/shard_map/ppermute | solution.py:527
  15.4 4.1 %collective-permute-done.3.refs_4_ = f32[96,128]{1,0:T(8,128)S(1)} collective-permute-done((f32[96,128]{1,0:T(8,128)S(1)}, f32[96,128]{1,0:T(8,128)S(1)}, u32[]{:S(2)}, u32[]{:S(2)}) %collective-permute-start.3) | collective-permute-done | bytes 49184 | tf_op jit(solution)/shard_map/ppermute | solution.py:526
  19.5 0.0 copy-done
  19.5 6.2 %step.1 = (f32[3,2,2,2,128]{4,3,2,1,0:T(2,128)}, f32[32,128]{1,0:T(8,128)S(1)}, f32[16,128]{1,0:T(8,128)S(1)}) custom-call(f32[64,128]{1,0:T(8,128)S(1)} %copy-done, f32[32,128]{1,0:T(8,128)S(1)} %collective-permute-done.refs_1_, f32[64,128]{1,0:T(8,128)S(1)} %collective-permute-done.1.refs_2_, f32[32,128]{1,0:T(8,128)S(1)} %collective-permute-done.2.refs_3_, ...), custom_call_target="tpu_custom_call" | custom-call | tf_op jit(solution)/shard_map/step/pallas_call | solution.py:557
  25.7 0.0 collective-permute-start.7
  25.7 0.6 %collective-permute-start.5 = (f32[16,128]{1,0:T(8,128)S(1)}, f32[16,128]{1,0:T(8,128)S(1)}, u32[]{:S(2)}, u32[]{:S(2)}) collective-permute-start(f32[16,128]{1,0:T(8,128)S(1)} %get-tuple-element.19), channel_id=1, source_target_pairs={{0,1},{1,0},{2,3},{3,2},{4,5},{5,4},{6,7},{7,6},{8,9},{9,8},{10,11... | collective-permute-start | bytes 24584 | tf_op jit(solution)/shard_map/ppermute | solution.py:488
  26.4 1.5 %collective-permute-start.6 = (f32[32,128]{1,0:T(8,128)S(1)}, f32[32,128]{1,0:T(8,128)S(1)}, u32[]{:S(2)}, u32[]{:S(2)}) collective-permute-start(f32[32,128]{1,0:T(8,128)S(1)} %get-tuple-element.18.refs_6_), channel_id=1, source_target_pairs={{0,2},{2,0},{1,3},{3,1},{4,6},{6,4},{5,7},{7,5},{8,10},{10,8},{9,1... | collective-permute-start | bytes 49160 | tf_op jit(solution)/shard_map/ppermute | solution.py:490
  27.9 0.9 %collective-permute-done.7.refs_9_ = f32[16,128]{1,0:T(8,128)S(1)} collective-permute-done((f32[16,128]{1,0:T(8,128)S(1)}, f32[16,128]{1,0:T(8,128)S(1)}, u32[]{:S(2)}, u32[]{:S(2)}) %collective-permute-start.7) | collective-permute-done | bytes 8224 | tf_op jit(solution)/shard_map/ppermute | solution.py:491
  28.8 0.0 collective-permute-done.5.refs_7_
  28.8 1.3 %collective-permute-done.6.refs_8_ = f32[32,128]{1,0:T(8,128)S(1)} collective-permute-done((f32[32,128]{1,0:T(8,128)S(1)}, f32[32,128]{1,0:T(8,128)S(1)}, u32[]{:S(2)}, u32[]{:S(2)}) %collective-permute-start.6) | collective-permute-done | bytes 16416 | tf_op jit(solution)/shard_map/ppermute | solution.py:490
  30.1 0.0 collective-permute-start.8
  30.2 3.8 %collective-permute-start.9 = (f32[48,128]{1,0:T(8,128)S(1)}, f32[48,128]{1,0:T(8,128)S(1)}, u32[]{:S(2)}, u32[]{:S(2)}) collective-permute-start(f32[48,128]{1,0:T(8,128)S(1)} %concatenate.15), channel_id=1, source_target_pairs={{0,12},{4,0},{8,4},{12,8},{1,13},{5,1},{9,5},{13,9},{2,14},{6,2},{... | collective-permute-start | bytes 73736 | tf_op jit(solution)/shard_map/ppermute | solution.py:527
  34.1 1.7 %collective-permute-done.8.refs_10_ = f32[48,128]{1,0:T(8,128)S(1)} collective-permute-done((f32[48,128]{1,0:T(8,128)S(1)}, f32[48,128]{1,0:T(8,128)S(1)}, u32[]{:S(2)}, u32[]{:S(2)}) %collective-permute-start.8) | collective-permute-done | bytes 24608 | tf_op jit(solution)/shard_map/ppermute | solution.py:526
  35.8 0.0 collective-permute-done.9.refs_11_
  35.8 8.5 %field.1 = (f32[3,2,2,2,128]{4,3,2,1,0:T(2,128)}, f32[16,128]{1,0:T(8,128)S(1)}) custom-call(f32[64,128]{1,0:T(8,128)S(1)} %copy-done, f32[32,128]{1,0:T(8,128)S(1)} %collective-permute-done.refs_1_, f32[64,128]{1,0:T(8,128)S(1)} %collective-permute-done.1.refs_2_, f32[32,128]{1,0:T(8,128)S(1)} %collective-permute-done.2.refs_3_, ...), custom_call_target="tpu_custom_call" | custom-call | tf_op jit(solution)/shard_map/field/pallas_call | solution.py:567
  44.3 0.0 copy-start.1
  44.3 14.2 %all_to_all.5.parts = f32[16,16,128]{2,1,0:T(8,128)S(1)} all-to-all(f32[16,16,128]{2,1,0:T(8,128)S(1)} %broadcast_in_dim.3), channel_id=1, replica_groups=mesh['groups'=2,'down'=4,'cross'=2,'depth'=2] {'down','cross','depth'}, dimensions={0} | all-to-all | bytes 262144 | tf_op jit(solution)/shard_map/all_to_all | solution.py:577
  58.4 0.0 copy-done.1
  58.4 1.5 %library.1 = (f32[2,2,2]{2,1,0:T(2,128)}, f32[48,48]{1,0:T(8,128)}, f32[1,48]{1,0:T(1,128)}) custom-call(f32[48]{0:T(128)S(1)} %copy-done.1, f32[16,16,128]{2,1,0:T(8,128)S(1)} %all_to_all.5.parts), custom_call_target="tpu_custom_call" | custom-call | tf_op jit(solution)/shard_map/library/pallas_call | solution.py:580
  (12 shorter events, 0.1 us)
Async XLA Ops:
  2.7 7.3 %collective-permute-start.2 = (f32[32,128]{1,0:T(8,128)}, f32[32,128]{1,0:T(8,128)S(1)}, u32[]{:S(2)}, u32[]{:S(2)}) collective-permute-start(f32[32,128]{1,0:T(8,128)} %get-tuple-element.16), channel_id=1, source_target_pairs={{0,3},{1,2},{2,1},{3,0},{4,7},{5,6},{6,5},{7,4},{8,11},{9,10},{10,... | collective-permute-start | bytes 49160 | tf_op jit(solution)/shard_map/ppermute | solution.py:491
  5.2 1.7 %collective-permute-start = (f32[32,128]{1,0:T(8,128)}, f32[32,128]{1,0:T(8,128)S(1)}, u32[]{:S(2)}, u32[]{:S(2)}) collective-permute-start(f32[32,128]{1,0:T(8,128)} %get-tuple-element.16), channel_id=1, source_target_pairs={{0,1},{1,0},{2,3},{3,2},{4,5},{5,4},{6,7},{7,6},{8,9},{9,8},{10,11... | collective-permute-start | bytes 49160 | tf_op jit(solution)/shard_map/ppermute | solution.py:488
  5.8 4.1 %collective-permute-start.1 = (f32[64,128]{1,0:T(8,128)}, f32[64,128]{1,0:T(8,128)S(1)}, u32[]{:S(2)}, u32[]{:S(2)}) collective-permute-start(f32[64,128]{1,0:T(8,128)} %get-tuple-element.15.refs_0_), channel_id=1, source_target_pairs={{0,2},{2,0},{1,3},{3,1},{4,6},{6,4},{5,7},{7,5},{8,10},{10,8},{9,1... | collective-permute-start | bytes 98312 | tf_op jit(solution)/shard_map/ppermute | solution.py:490
  10.0 9.6 %copy-start = (f32[64,128]{1,0:T(8,128)S(1)}, f32[64,128]{1,0:T(8,128)}, u32[]{:S(2)}) copy-start(f32[64,128]{1,0:T(8,128)} %get-tuple-element.15.refs_0_) | copy-start | bytes 98308
  10.0 5.4 %collective-permute-start.4 = (f32[96,128]{1,0:T(8,128)S(1)}, f32[96,128]{1,0:T(8,128)S(1)}, u32[]{:S(2)}, u32[]{:S(2)}) collective-permute-start(f32[96,128]{1,0:T(8,128)S(1)} %get-tuple-element.37), channel_id=1, source_target_pairs={{0,12},{4,0},{8,4},{12,8},{1,13},{5,1},{9,5},{13,9},{2,14},{6,2},{... | collective-permute-start | bytes 147464 | tf_op jit(solution)/shard_map/ppermute | solution.py:527
  13.7 5.9 %collective-permute-start.3 = (f32[96,128]{1,0:T(8,128)S(1)}, f32[96,128]{1,0:T(8,128)S(1)}, u32[]{:S(2)}, u32[]{:S(2)}) collective-permute-start(f32[96,128]{1,0:T(8,128)S(1)} %get-tuple-element.38), channel_id=1, source_target_pairs={{0,4},{4,8},{8,12},{12,0},{1,5},{5,9},{9,13},{13,1},{2,6},{6,10},{... | collective-permute-start | bytes 147464 | tf_op jit(solution)/shard_map/ppermute | solution.py:526
  25.7 3.1 %collective-permute-start.7 = (f32[16,128]{1,0:T(8,128)S(1)}, f32[16,128]{1,0:T(8,128)S(1)}, u32[]{:S(2)}, u32[]{:S(2)}) collective-permute-start(f32[16,128]{1,0:T(8,128)S(1)} %get-tuple-element.19), channel_id=1, source_target_pairs={{0,3},{1,2},{2,1},{3,0},{4,7},{5,6},{6,5},{7,4},{8,11},{9,10},{10,... | collective-permute-start | bytes 24584 | tf_op jit(solution)/shard_map/ppermute | solution.py:491
  25.7 3.1 %collective-permute-start.5 = (f32[16,128]{1,0:T(8,128)S(1)}, f32[16,128]{1,0:T(8,128)S(1)}, u32[]{:S(2)}, u32[]{:S(2)}) collective-permute-start(f32[16,128]{1,0:T(8,128)S(1)} %get-tuple-element.19), channel_id=1, source_target_pairs={{0,1},{1,0},{2,3},{3,2},{4,5},{5,4},{6,7},{7,6},{8,9},{9,8},{10,11... | collective-permute-start | bytes 24584 | tf_op jit(solution)/shard_map/ppermute | solution.py:488
  26.4 3.7 %collective-permute-start.6 = (f32[32,128]{1,0:T(8,128)S(1)}, f32[32,128]{1,0:T(8,128)S(1)}, u32[]{:S(2)}, u32[]{:S(2)}) collective-permute-start(f32[32,128]{1,0:T(8,128)S(1)} %get-tuple-element.18.refs_6_), channel_id=1, source_target_pairs={{0,2},{2,0},{1,3},{3,1},{4,6},{6,4},{5,7},{7,5},{8,10},{10,8},{9,1... | collective-permute-start | bytes 49160 | tf_op jit(solution)/shard_map/ppermute | solution.py:490
  30.1 5.7 %collective-permute-start.8 = (f32[48,128]{1,0:T(8,128)S(1)}, f32[48,128]{1,0:T(8,128)S(1)}, u32[]{:S(2)}, u32[]{:S(2)}) collective-permute-start(f32[48,128]{1,0:T(8,128)S(1)} %concatenate.14), channel_id=1, source_target_pairs={{0,4},{4,8},{8,12},{12,0},{1,5},{5,9},{9,13},{13,1},{2,6},{6,10},{... | collective-permute-start | bytes 73736 | tf_op jit(solution)/shard_map/ppermute | solution.py:526
  30.2 5.6 %collective-permute-start.9 = (f32[48,128]{1,0:T(8,128)S(1)}, f32[48,128]{1,0:T(8,128)S(1)}, u32[]{:S(2)}, u32[]{:S(2)}) collective-permute-start(f32[48,128]{1,0:T(8,128)S(1)} %concatenate.15), channel_id=1, source_target_pairs={{0,12},{4,0},{8,4},{12,8},{1,13},{5,1},{9,5},{13,9},{2,14},{6,2},{... | collective-permute-start | bytes 73736 | tf_op jit(solution)/shard_map/ppermute | solution.py:527
  44.3 14.2 %copy-start.1 = (f32[48]{0:T(128)S(1)}, f32[48]{0:T(128)}, u32[]{:S(2)}) copy-start(f32[48]{0:T(128)} %coefficients.1) | copy-start | bytes 580

commit v2 on v1

--- a/solution.py
+++ b/solution.py
@@ -58,7 +58,7 @@
 
 
 def pack_kernel(
-    counts, positions_hbm, velocities_hbm, radii_hbm, own, inner, positions, velocities, radii, arrived
+    counts, positions_hbm, velocities_hbm, radii_hbm, own, positions, velocities, radii, arrived
 ):
     copies = [
         pltpu.make_async_copy(source, target, arrived.at[k])
@@ -70,7 +70,6 @@
         copy.start()
     for copy in copies:
         copy.wait()
-    depth = lax.axis_index("depth")
     lanes = lane_ids((1, S))
     for c, (a, b, z) in enumerate(CELLS):
         for k in range(3):
@@ -79,9 +78,6 @@
         live = lanes < counts[a, b, z]
         own[c * 8 + 6 : c * 8 + 7, :] = jnp.where(live, radii[a, b, z : z + 1, :], DEAD)
         own[c * 8 + 7 : c * 8 + 8, :] = jnp.zeros((1, S), F32)
-    for column in range(4):
-        source = pl.multiple_of(column * 16 + (1 - depth) * 8, 8)
-        inner[column * 8 : column * 8 + 8, :] = own[pl.ds(source, 8), :]
 
 
 def local_state(raw, centre):
@@ -90,31 +86,20 @@
     return jnp.where(rows < 3, raw + shift, raw)
 
 
-def piece_reader(refs, wide, height):
-    own, depth_halo = refs[0], refs[1]
-    x_before, x_after = refs[-2], refs[-1]
-
-    def read(ref, cell):
-        return ref[cell * height : cell * height + height, :]
+def cell_reader(gathered, height):
+    down, cross, depth = (lax.axis_index(name) for name in ("down", "cross", "depth"))
+    downs, crosses = lax.axis_size("down"), lax.axis_size("cross")
 
     def cell(x, y, slot):
-        if x in (0, 3):
-            face = x_before if x == 0 else x_after
-            if y in (1, 2):
-                return read(face, (y - 1) * 2 + slot if slot < 2 else 4 + y - 1)
-            side = 0 if y == 0 else 1
-            return read(face, 6 + side * 2 + slot if slot < 2 else 10 + side)
-        a = x - 1
-        if y in (1, 2):
-            return read(own, a * 4 + (y - 1) * 2 + slot) if slot < 2 else read(depth_halo, a * 2 + y - 1)
-        if wide:
-            before, after, diag_before, diag_after = refs[2:6]
-            if slot < 2:
-                return read(before if y == 0 else after, a * 2 + slot)
-            return read(diag_before if y == 0 else diag_after, a)
-        side, diag = refs[2:4]
-        b = 1 if y == 0 else 0
-        return read(side, a * 4 + b * 2 + slot) if slot < 2 else read(diag, a * 2 + b)
+        down_at = lax.rem(down + (x + 1) // 2 - 1 + downs, downs)
+        cross_at = lax.rem(cross + (y + 1) // 2 - 1 + crosses, crosses)
+        device = (down_at * crosses + cross_at) * 2
+        place = (1 - x % 2) * 4 + (1 - y % 2) * 2
+        if slot < 2:
+            start = (device + depth) * 8 + place + slot
+        else:
+            start = (device + 1 - depth) * 8 + place + depth
+        return gathered[pl.ds(pl.multiple_of(start * height, height), height), :]
 
     return cell
 
@@ -265,13 +250,9 @@
     return scaled * scaled * scaled
 
 
-def step_kernel(wide, *refs):
-    count = 8 if wide else 6
-    pieces, (velocity_out, own_out, inner_out) = refs[:count], refs[count : count + 3]
-    scratch = refs[count + 3 :]
-    own = pieces[0]
+def step_kernel(own, gathered, velocity_out, own_out, *scratch):
     depth = lax.axis_index("depth")
-    cell = piece_reader(pieces, wide, 8)
+    cell = cell_reader(gathered, 8)
     for x, y, slot, start, centre in extended_cells(depth):
         scratch[0][start : start + 8, :] = local_state(cell(x, y, slot), centre)
     sums = contact_all(depth, 3, scratch)
@@ -285,23 +266,15 @@
                 velocity_out[k, a, b, :, :] = velocity[c : c + 2]
     for c in range(8):
         own_out[c * 4 + 3 : c * 4 + 4, :] = jnp.zeros((1, S), F32)
-    for column in range(4):
-        chosen = own_out[column * 8 : column * 8 + 8, :]
-        inner_out[column * 4 : column * 4 + 4, :] = jnp.where(depth == 0, chosen[4:8], chosen[0:4])
-
-
-def field_kernel(wide, grid, *refs):
-    count = 8 if wide else 6
-    pieces, speeds = refs[:count], refs[count : 2 * count]
-    force_out, node_out = refs[2 * count : 2 * count + 2]
-    moment_ref = refs[2 * count + 2]
-    scratch = refs[2 * count + 3 :]
+
+
+def field_kernel(grid, own, gathered, own_speed, speeds, force_out, node_out, moment_ref, *scratch):
     local_ref = scratch[0]
     depth = lax.axis_index("depth")
     down = lax.axis_index("down")
     cross = lax.axis_index("cross")
-    cell = piece_reader(pieces, wide, 8)
-    speed = piece_reader(speeds, wide, 4)
+    cell = cell_reader(gathered, 8)
+    speed = cell_reader(speeds, 4)
     for x, y, slot, start, centre in extended_cells(depth):
         old = cell(x, y, slot)
         new = speed(x, y, slot)[0:3]
@@ -312,9 +285,9 @@
         local_ref[start + 3 : start + 6, :] = new
         local_ref[start + 6 : start + 8, :] = old[6:8]
     sums = contact_all(depth, 9, scratch)
-    radius = pieces[0][pl.ds(6, 8, stride=8), :]
+    radius = own[pl.ds(6, 8, stride=8), :]
     mass = jnp.where(radius > 0.0, mass_of(radius), 0.0)
-    moments = [mass] + [mass * speeds[0][pl.ds(k, 8, stride=4), :] for k in range(3)]
+    moments = [mass] + [mass * own_speed[pl.ds(k, 8, stride=4), :] for k in range(3)]
     moments += [0.5 * sums[k * 8 : k * 8 + 8] for k in range(3, 9)]
     moment_ref[...] = jnp.zeros((16, 8 * S), F32)
     for k in range(3):
@@ -474,63 +447,12 @@
         residual_out[a] = jnp.where(z_lanes == 0, column[0], column[1])
 
 
-def ring(axis, step):
-    peers = lax.axis_size(axis)
-    return [(i, (i + step) % peers) for i in range(peers)]
-
-
-def exchange(own, inner, height):
-    cross = lax.axis_size("cross")
-
-    def cells(block, first, count):
-        return block[first * height : (first + count) * height]
-
-    depth_halo = lax.ppermute(inner, "depth", [(0, 1), (1, 0)])
-    if cross == 2:
-        side = lax.ppermute(own, "cross", [(0, 1), (1, 0)])
-        diag = lax.ppermute(inner, ("cross", "depth"), [(i, 3 - i) for i in range(4)])
-        sides = [side, diag]
-
-        def lateral(x):
-            return [
-                cells(side, x * 4 + 2, 2),
-                cells(side, x * 4, 2),
-                cells(diag, x * 2 + 1, 1),
-                cells(diag, x * 2, 1),
-            ]
-
-    else:
-        pairs = [(i * 2 + j, ((i + 1) % cross) * 2 + 1 - j) for i in range(cross) for j in range(2)]
-        back = [(i * 2 + j, ((i - 1) % cross) * 2 + 1 - j) for i in range(cross) for j in range(2)]
-        last = jnp.concatenate([cells(own, 2, 2), cells(own, 6, 2)], axis=0)
-        first = jnp.concatenate([cells(own, 0, 2), cells(own, 4, 2)], axis=0)
-        last_inner = jnp.concatenate([cells(inner, 1, 1), cells(inner, 3, 1)], axis=0)
-        first_inner = jnp.concatenate([cells(inner, 0, 1), cells(inner, 2, 1)], axis=0)
-        before = lax.ppermute(last, "cross", ring("cross", 1))
-        after = lax.ppermute(first, "cross", ring("cross", -1))
-        diag_before = lax.ppermute(last_inner, ("cross", "depth"), pairs)
-        diag_after = lax.ppermute(first_inner, ("cross", "depth"), back)
-        sides = [before, after, diag_before, diag_after]
-
-        def lateral(x):
-            return [
-                cells(before, x * 2, 2),
-                cells(after, x * 2, 2),
-                cells(diag_before, x, 1),
-                cells(diag_after, x, 1),
-            ]
-
-    def face(x):
-        return jnp.concatenate([cells(own, x * 4, 4), cells(depth_halo, x * 2, 2)] + lateral(x), axis=0)
-
-    x_before = lax.ppermute(face(1), "down", ring("down", 1))
-    x_after = lax.ppermute(face(0), "down", ring("down", -1))
-    return [own, depth_halo] + sides + [x_before, x_after]
+def gather(value):
+    return lax.all_gather(value, ("down", "cross", "depth"), tiled=True)
 
 
 def body(positions, velocities, sphere_radii, counts, coefficients):
     down, cross, depth = (lax.axis_size(name) for name in ("down", "cross", "depth"))
-    wide = cross != 2
     grid = (2 * down, 2 * cross, 2 * depth)
     nodes = grid[0] * grid[1] * grid[2]
     params = pltpu.CompilerParams(vmem_limit_bytes=VMEM_LIMIT)
@@ -539,11 +461,11 @@
     def rows(count):
         return jax.ShapeDtypeStruct((count, S), F32)
 
-    own, inner = pl.pallas_call(
+    own = pl.pallas_call(
         pack_kernel,
-        out_shape=(rows(64), rows(32)),
+        out_shape=rows(64),
         in_specs=[SMEM_SPEC] + [pl.BlockSpec(memory_space=pl.ANY)] * 3,
-        out_specs=(VMEM_SPEC, VMEM_SPEC),
+        out_specs=VMEM_SPEC,
         scratch_shapes=[
             pltpu.VMEM((3, 2, 2, 2, S), F32),
             pltpu.VMEM((3, 2, 2, 2, S), F32),
@@ -553,30 +475,27 @@
         compiler_params=pltpu.CompilerParams(vmem_limit_bytes=60 * 1024 * 1024),
         name="pack",
     )(counts, positions, velocities, sphere_radii)
-    pieces = exchange(own, inner, 8)
-    velocity_new, own_speed, inner_speed = pl.pallas_call(
-        functools.partial(step_kernel, wide),
-        out_shape=(vector_shape, rows(32), rows(16)),
-        in_specs=[VMEM_SPEC] * len(pieces),
-        out_specs=(VMEM_SPEC,) * 3,
+    gathered = gather(own)
+    velocity_new, own_speed = pl.pallas_call(
+        step_kernel,
+        out_shape=(vector_shape, rows(32)),
+        in_specs=[VMEM_SPEC] * 2,
+        out_specs=(VMEM_SPEC,) * 2,
         scratch_shapes=contact_scratch(3),
         compiler_params=params,
         name="step",
-    )(*pieces)
-    speeds = exchange(own_speed, inner_speed, 4)
+    )(own, gathered)
+    speeds = gather(own_speed)
     force_next, partial = pl.pallas_call(
-        functools.partial(field_kernel, wide, grid),
+        functools.partial(field_kernel, grid),
         out_shape=(vector_shape, jax.ShapeDtypeStruct((16, nodes), F32)),
-        in_specs=[VMEM_SPEC] * (len(pieces) + len(speeds)),
+        in_specs=[VMEM_SPEC] * 4,
         out_specs=(VMEM_SPEC,) * 2,
         scratch_shapes=[pltpu.VMEM((16, 8 * S), F32)] + contact_scratch(9),
         compiler_params=params,
         name="field",
-    )(*pieces, *speeds)
-    peers = down * cross * depth
-    parts = lax.all_to_all(
-        jnp.broadcast_to(partial, (peers, 16, nodes)), ("down", "cross", "depth"), 0, 0
-    )
+    )(own, gathered, own_speed, speeds)
+    parts = gather(partial).reshape(down * cross * depth, 16, nodes)
     residual_field, gram_matrix, moment = pl.pallas_call(
         functools.partial(library_kernel, grid),
         out_shape=(

time: 60.4 us -> 81.5 us (1.35)
  blocking collectives: 14.2 us -> 61.9 us
  waiting for transfers between devices: 13.2 us -> 0 us
  starting transfers between devices: 12.9 us -> 0 us
  Pallas kernels: 18.2 us -> 17 us
    all_gather x0 -> x3, blocking collectives: none -> 61.9 us  [gather(): return lax.all_gather(value, ('down', 'cross', 'depth'), tiled=True)]
    all_to_all x1 -> x0, blocking collectives: 14.2 us -> none  [body(): lax.all_to_all(jnp.broadcast_to(partial, (peers, 16, nodes)), ('down', 'c...]
    ppermute x10 -> x0, waiting for transfers between devices: 13.2 us -> none  [the longest x2 5.87 us: exchange(): x_before = lax.ppermute(face(1), 'down', ring('down', 1))]
    ppermute x10 -> x0, starting transfers between devices: 12.9 us -> none  [the longest x2 7.5 us: exchange(): x_after = lax.ppermute(face(0), 'down', ring('down', -1))]
    pallas_call x3, Pallas kernels: 16.7 us -> 15.5 us  [the longest x1 7.41 us: body(): pl.pallas_call(functools.partial(field_kernel, grid), out_shape=(vector_s...]
  transfers between devices with their start and end apart: 10 -> 0, of which waited for: 7 -> 0; matrix products, arithmetic and copies ran while one was open for 1% -> 0% of each run, Pallas kernels for 0% -> 0%
where the time goes in v2:
time: 81.5 us; the launch traced here: 80.2 us
  blocking collectives  61.9 us (76%)
  Pallas kernels  17 us (21%)
    all_gather x3, blocking collectives, gather(): return lax.all_gather(value, ('down', 'cross', 'depth'), tiled=True)  61.9 us
    pallas_call x1, Pallas kernels, body(): pl.pallas_call(functools.partial(field_kernel, grid), out_shape=(vector_s...  7.41 us
    pallas_call x1, Pallas kernels, body(): pl.pallas_call(step_kernel, out_shape=(vector_shape, rows(32)), in_specs=...  6.02 us
    pallas_call x1, Pallas kernels, body(): pl.pallas_call(pack_kernel, out_shape=rows(64), in_specs=[SMEM_SPEC] + [p...  2.07 us

profile of v2, /device:TPU:0, one launch (start us, length us, event | category | flops | bytes accessed | tf_op | source)
XLA Modules:
  0.0 80.2 jit_solution(939559303250903619)
XLA Ops:
  0.6 2.1 %pack.1.own = f32[64,128]{1,0:T(8,128)} custom-call(s32[2,2,2]{2,1,0:T(2,128)} %counts.1, f32[3,2,2,2,128]{4,3,2,1,0:T(2,128)} %positions_hbm.1, f32[3,2,2,2,128]{4,3,2,1,0:T(2,128)} %velocities_hbm.1, f32[2,2,2,128]{3,2,1,0:T(2,128)} %radii_hbm.1), custom_call_target="tpu_custom_call" | custom-call | tf_op jit(solution)/shard_map/pack/pallas_call | solution.py:464
  2.7 0.0 copy-start
  2.7 24.8 %all_gather.9.gathered = f32[1024,128]{1,0:T(8,128)S(1)} all-gather(f32[64,128]{1,0:T(8,128)} %pack.1.own), channel_id=1, replica_groups=mesh['groups'=2,'down'=4,'cross'=2,'depth'=2] {'down','cross','depth'}, dimensions={0}, use_global_device_ids=true | all-gather | bytes 557056 | tf_op jit(solution)/shard_map/all_gather | solution.py:451
  27.5 0.0 copy-done
  27.5 6.0 %step.1 = (f32[3,2,2,2,128]{4,3,2,1,0:T(2,128)}, f32[32,128]{1,0:T(8,128)S(1)}) custom-call(f32[64,128]{1,0:T(8,128)S(1)} %copy-done, f32[1024,128]{1,0:T(8,128)S(1)} %all_gather.9.gathered), custom_call_target="tpu_custom_call" | custom-call | tf_op jit(solution)/shard_map/step/pallas_call | solution.py:479
  33.5 17.8 %all_gather.10.speeds = f32[512,128]{1,0:T(8,128)S(1)} all-gather(f32[32,128]{1,0:T(8,128)S(1)} %get-tuple-element.13.own_speed), channel_id=1, replica_groups=mesh['groups'=2,'down'=4,'cross'=2,'depth'=2] {'down','cross','depth'}, dimensions={0}, use_global_device_ids=true | all-gather | bytes 278528 | tf_op jit(solution)/shard_map/all_gather | solution.py:451
  51.4 7.4 %field.1 = (f32[3,2,2,2,128]{4,3,2,1,0:T(2,128)}, f32[16,128]{1,0:T(8,128)S(1)}) custom-call(f32[64,128]{1,0:T(8,128)S(1)} %copy-done, f32[1024,128]{1,0:T(8,128)S(1)} %all_gather.9.gathered, f32[32,128]{1,0:T(8,128)S(1)} %get-tuple-element.13.own_speed, f32[512,128]{1,0:T(8,128)S(1)} %all_gather.10.speeds), custom_call_target="tpu_custom_call" | custom-call | tf_op jit(solution)/shard_map/field/pallas_call | solution.py:489
  58.8 19.3 %all_gather.11 = f32[256,128]{1,0:T(8,128)S(1)} all-gather(f32[16,128]{1,0:T(8,128)S(1)} %get-tuple-element.15), channel_id=1, replica_groups=mesh['groups'=2,'down'=4,'cross'=2,'depth'=2] {'down','cross','depth'}, dimensions={0}, use_global_device_ids=true | all-gather | bytes 139264 | tf_op jit(solution)/shard_map/all_gather | solution.py:451
  78.1 0.0 copy-start.1
  78.1 0.7 copy-done.1
  78.8 1.5 %library.1 = (f32[2,2,2]{2,1,0:T(2,128)}, f32[48,48]{1,0:T(8,128)}, f32[1,48]{1,0:T(1,128)}) custom-call(f32[48]{0:T(128)S(1)} %copy-done.1, f32[16,16,128]{2,1,0:T(8,128)S(1)} %bitcast.2), custom_call_target="tpu_custom_call" | custom-call | tf_op jit(solution)/shard_map/library/pallas_call | solution.py:499
Async XLA Ops:
  2.7 24.8 %copy-start = (f32[64,128]{1,0:T(8,128)S(1)}, f32[64,128]{1,0:T(8,128)}, u32[]{:S(2)}) copy-start(f32[64,128]{1,0:T(8,128)} %pack.1.own) | copy-start | bytes 98308
  78.1 0.7 copy-start.1

commit v3 on v1

--- a/solution.py
+++ b/solution.py
@@ -92,14 +92,21 @@
 
 def piece_reader(refs, wide, height):
     own, depth_halo = refs[0], refs[1]
+    downs = lax.axis_size("down")
     x_before, x_after = refs[-2], refs[-1]
 
     def read(ref, cell):
+        if isinstance(ref, int):
+            peer = lax.rem(lax.axis_index("down") + ref + downs, downs)
+            start = pl.multiple_of(peer * (12 * height) + cell * height, height)
+            return refs[-1][pl.ds(start, height), :]
         return ref[cell * height : cell * height + height, :]
 
     def cell(x, y, slot):
         if x in (0, 3):
             face = x_before if x == 0 else x_after
+            if downs in (3, 4):
+                face = -1 if x == 0 else 1
             if y in (1, 2):
                 return read(face, (y - 1) * 2 + slot if slot < 2 else 4 + y - 1)
             side = 0 if y == 0 else 1
@@ -265,8 +272,7 @@
     return scaled * scaled * scaled
 
 
-def step_kernel(wide, *refs):
-    count = 8 if wide else 6
+def step_kernel(count, wide, *refs):
     pieces, (velocity_out, own_out, inner_out) = refs[:count], refs[count : count + 3]
     scratch = refs[count + 3 :]
     own = pieces[0]
@@ -290,8 +296,7 @@
         inner_out[column * 4 : column * 4 + 4, :] = jnp.where(depth == 0, chosen[4:8], chosen[0:4])
 
 
-def field_kernel(wide, grid, *refs):
-    count = 8 if wide else 6
+def field_kernel(count, wide, grid, *refs):
     pieces, speeds = refs[:count], refs[count : 2 * count]
     force_out, node_out = refs[2 * count : 2 * count + 2]
     moment_ref = refs[2 * count + 2]
@@ -479,6 +484,13 @@
     return [(i, (i + step) % peers) for i in range(peers)]
 
 
+def spread_along_down(last, first):
+    downs = lax.axis_size("down")
+    me = lax.axis_index("down")
+    chunks = [jnp.where(lax.rem(me + 1, downs) == k, last, first) for k in range(downs)]
+    return lax.all_to_all(jnp.concatenate(chunks, axis=0), "down", 0, 0, tiled=True)
+
+
 def exchange(own, inner, height):
     cross = lax.axis_size("cross")
 
@@ -523,9 +535,23 @@
     def face(x):
         return jnp.concatenate([cells(own, x * 4, 4), cells(depth_halo, x * 2, 2)] + lateral(x), axis=0)
 
+    if lax.axis_size("down") in (3, 4):
+        return [own, depth_halo] + sides + [spread_along_down(face(1), face(0))]
     x_before = lax.ppermute(face(1), "down", ring("down", 1))
     x_after = lax.ppermute(face(0), "down", ring("down", -1))
     return [own, depth_halo] + sides + [x_before, x_after]
+
+
+def shared(value, axes, peers):
+    return [value] + [
+        lax.ppermute(value, axes, [(i, i ^ k) for i in range(peers)]) for k in range(1, peers)
+    ]
+
+
+def tree_sum(parts):
+    while len(parts) > 1:
+        parts = [parts[k] + parts[k + 1] for k in range(0, len(parts), 2)]
+    return parts[0]
 
 
 def body(positions, velocities, sphere_radii, counts, coefficients):
@@ -555,7 +581,7 @@
     )(counts, positions, velocities, sphere_radii)
     pieces = exchange(own, inner, 8)
     velocity_new, own_speed, inner_speed = pl.pallas_call(
-        functools.partial(step_kernel, wide),
+        functools.partial(step_kernel, len(pieces), wide),
         out_shape=(vector_shape, rows(32), rows(16)),
         in_specs=[VMEM_SPEC] * len(pieces),
         out_specs=(VMEM_SPEC,) * 3,
@@ -565,7 +591,7 @@
     )(*pieces)
     speeds = exchange(own_speed, inner_speed, 4)
     force_next, partial = pl.pallas_call(
-        functools.partial(field_kernel, wide, grid),
+        functools.partial(field_kernel, len(pieces), wide, grid),
         out_shape=(vector_shape, jax.ShapeDtypeStruct((16, nodes), F32)),
         in_specs=[VMEM_SPEC] * (len(pieces) + len(speeds)),
         out_specs=(VMEM_SPEC,) * 2,
@@ -573,10 +599,8 @@
         compiler_params=params,
         name="field",
     )(*pieces, *speeds)
-    peers = down * cross * depth
-    parts = lax.all_to_all(
-        jnp.broadcast_to(partial, (peers, 16, nodes)), ("down", "cross", "depth"), 0, 0
-    )
+    partial = tree_sum(shared(partial, ("cross", "depth"), cross * depth))
+    parts = lax.all_to_all(jnp.broadcast_to(partial, (down, 16, nodes)), "down", 0, 0)
     residual_field, gram_matrix, moment = pl.pallas_call(
         functools.partial(library_kernel, grid),
         out_shape=(

time: 60.4 us -> 62.8 us (1.040)
  blocking collectives: 14.2 us -> 27.9 us
  waiting for transfers between devices: 13.2 us -> 7.31 us
  starting transfers between devices: 12.9 us -> 8.25 us
  Pallas kernels: 18.2 us -> 16.8 us
    all_to_all x1 -> x3, blocking collectives: 14.2 us -> 27.9 us  [the longest x2 19.7 us: spread_along_down(): lax.all_to_all(jnp.concatenate(chunks, axis=0), 'down', 0, 0, tiled=True)]
    ppermute x4 -> x3, waiting for transfers between devices: 7.62 us -> 1.6 us  [shared(): lax.ppermute(value, axes, [(i, i ^ k) for i in range(peers)])]
    ppermute x4 -> x3, starting transfers between devices: 7.55 us -> 2.95 us  [shared(): lax.ppermute(value, axes, [(i, i ^ k) for i in range(peers)])]
    pallas_call x2, Pallas kernels: 14.6 us -> 13.2 us  [the longest x1 7.2 us: body(): pl.pallas_call(functools.partial(field_kernel, len(pieces), wide, grid),...]
  transfers between devices with their start and end apart: 10 -> 9, of which waited for: 7 -> 6; matrix products, arithmetic and copies ran while one was open for 1% -> 1% of each run, Pallas kernels for 0% -> 0%
where the time goes in v3:
time: 62.8 us; the launch traced here: 61.8 us
  blocking collectives  27.9 us (44%)
  Pallas kernels  16.8 us (27%)
  starting transfers between devices  8.25 us (13%)
  waiting for transfers between devices  7.31 us (12%)
  local copies, waits for them, and re-layouts  0.84 us (1%)
  between operations  0.73 us (1%)
    all_to_all x2, blocking collectives, spread_along_down(): lax.all_to_all(jnp.concatenate(chunks, axis=0), 'down', 0, 0, tiled=True)  19.7 us
    all_to_all x1, blocking collectives, body(): lax.all_to_all(jnp.broadcast_to(partial, (down, 16, nodes)), 'down', 0, 0)  8.21 us
    pallas_call x1, Pallas kernels, body(): pl.pallas_call(functools.partial(field_kernel, len(pieces), wide, grid),...  7.2 us
    pallas_call x1, Pallas kernels, body(): pl.pallas_call(functools.partial(step_kernel, len(pieces), wide), out_sha...  6.01 us
    ppermute x2, waiting for transfers between devices, exchange(): side = lax.ppermute(own, 'cross', [(0, 1), (1, 0)])  4.52 us
    ppermute x3, starting transfers between devices, shared(): lax.ppermute(value, axes, [(i, i ^ k) for i in range(peers)])  2.95 us
    ppermute x2, starting transfers between devices, exchange(): lax.ppermute(inner, ('cross', 'depth'), [(i, 3 - i) for i in range(4)])  2.45 us
    pallas_call x1, Pallas kernels, body(): pl.pallas_call(pack_kernel, out_shape=(rows(64), rows(32)), in_specs=[SME...  2.08 us
  transfers between devices with their start and end apart: 9, of which 6 were waited for; matrix products, arithmetic and copies ran while one was open for 1% of the time, Pallas kernels for 0%

profile of v3, /device:TPU:0, one launch (start us, length us, event | category | flops | bytes accessed | tf_op | source)
XLA Modules:
  0.0 61.8 jit_solution(5814846601191163857)
XLA Ops:
  0.6 2.1 %pack.1 = (f32[64,128]{1,0:T(8,128)}, f32[32,128]{1,0:T(8,128)}) custom-call(s32[2,2,2]{2,1,0:T(2,128)} %counts.1, f32[3,2,2,2,128]{4,3,2,1,0:T(2,128)} %positions_hbm.1, f32[3,2,2,2,128]{4,3,2,1,0:T(2,128)} %velocities_hbm.1, f32[2,2,2,128]{3,2,1,0:T(2,128)} %radii_hbm.1), custom_call_target="tpu_custom_call" | custom-call | tf_op jit(solution)/shard_map/pack/pallas_call | solution.py:568
  2.7 2.4 %collective-permute-start.2 = (f32[32,128]{1,0:T(8,128)}, f32[32,128]{1,0:T(8,128)S(1)}, u32[]{:S(2)}, u32[]{:S(2)}) collective-permute-start(f32[32,128]{1,0:T(8,128)} %get-tuple-element.16), channel_id=1, source_target_pairs={{0,3},{1,2},{2,1},{3,0},{4,7},{5,6},{6,5},{7,4},{8,11},{9,10},{10,... | collective-permute-start | bytes 49160 | tf_op jit(solution)/shard_map/ppermute | solution.py:503
  5.2 0.7 %collective-permute-start = (f32[32,128]{1,0:T(8,128)}, f32[32,128]{1,0:T(8,128)S(1)}, u32[]{:S(2)}, u32[]{:S(2)}) collective-permute-start(f32[32,128]{1,0:T(8,128)} %get-tuple-element.16), channel_id=1, source_target_pairs={{0,1},{1,0},{2,3},{3,2},{4,5},{5,4},{6,7},{7,6},{8,9},{9,8},{10,11... | collective-permute-start | bytes 49160 | tf_op jit(solution)/shard_map/ppermute | solution.py:500
  5.8 0.0 collective-permute-start.1
  5.9 0.8 %constant_dynamic-update-slice_fusion.11 = (f32[96,128]{1,0:T(8,128)S(1)}, f32[96,128]{1,0:T(8,128)S(1)}) fusion(f32[64,128]{1,0:T(8,128)} %get-tuple-element.15.refs_0_), kind=kLoop, calls=%fused_computation.13 | loop fusion | bytes 65536
  6.6 0.3 collective-permute-done.refs_1_
  6.9 3.1 %collective-permute-done.1.refs_2_ = f32[64,128]{1,0:T(8,128)S(1)} collective-permute-done((f32[64,128]{1,0:T(8,128)}, f32[64,128]{1,0:T(8,128)S(1)}, u32[]{:S(2)}, u32[]{:S(2)}) %collective-permute-start.1) | collective-permute-done | bytes 32800 | tf_op jit(solution)/shard_map/ppermute | solution.py:502
  10.0 0.0 collective-permute-done.2.refs_3_
  10.1 0.0 copy-start
  10.1 11.5 %all_to_all.27 = f32[4,96,128]{2,1,0:T(8,128)S(1)} all-to-all(f32[4,96,128]{2,1,0:T(8,128)S(1)} %bitcast.8), channel_id=1, replica_groups=mesh['groups'=2,'down'=4,'cross'=2,'depth'=2] {'down'}, dimensions={0} | all-to-all | bytes 393216 | tf_op jit(solution)/shard_map/all_to_all | solution.py:491
  21.5 0.0 copy-done
  21.5 6.0 %step.1 = (f32[3,2,2,2,128]{4,3,2,1,0:T(2,128)}, f32[32,128]{1,0:T(8,128)S(1)}, f32[16,128]{1,0:T(8,128)S(1)}) custom-call(f32[64,128]{1,0:T(8,128)S(1)} %copy-done, f32[32,128]{1,0:T(8,128)S(1)} %collective-permute-done.refs_1_, f32[64,128]{1,0:T(8,128)S(1)} %collective-permute-done.1.refs_2_, f32[32,128]{1,0:T(8,128)S(1)} %collective-permute-done.2.refs_3_, ...), custom_call_target="tpu_custom_call" | custom-call | tf_op jit(solution)/shard_map/step/pallas_call | solution.py:583
  27.5 0.0 collective-permute-start.5
  27.5 0.8 %collective-permute-start.3 = (f32[16,128]{1,0:T(8,128)S(1)}, f32[16,128]{1,0:T(8,128)S(1)}, u32[]{:S(2)}, u32[]{:S(2)}) collective-permute-start(f32[16,128]{1,0:T(8,128)S(1)} %get-tuple-element.19), channel_id=1, source_target_pairs={{0,1},{1,0},{2,3},{3,2},{4,5},{5,4},{6,7},{7,6},{8,9},{9,8},{10,11... | collective-permute-start | bytes 24584 | tf_op jit(solution)/shard_map/ppermute | solution.py:500
  28.3 1.3 %collective-permute-start.4 = (f32[32,128]{1,0:T(8,128)S(1)}, f32[32,128]{1,0:T(8,128)S(1)}, u32[]{:S(2)}, u32[]{:S(2)}) collective-permute-start(f32[32,128]{1,0:T(8,128)S(1)} %get-tuple-element.18.refs_5_), channel_id=1, source_target_pairs={{0,2},{2,0},{1,3},{3,1},{4,6},{6,4},{5,7},{7,5},{8,10},{10,8},{9,1... | collective-permute-start | bytes 49160 | tf_op jit(solution)/shard_map/ppermute | solution.py:502
  29.7 0.9 %collective-permute-done.5.refs_8_ = f32[16,128]{1,0:T(8,128)S(1)} collective-permute-done((f32[16,128]{1,0:T(8,128)S(1)}, f32[16,128]{1,0:T(8,128)S(1)}, u32[]{:S(2)}, u32[]{:S(2)}) %collective-permute-start.5) | collective-permute-done | bytes 8224 | tf_op jit(solution)/shard_map/ppermute | solution.py:503
  30.6 0.0 collective-permute-done.3.refs_6_
  30.6 1.4 %collective-permute-done.4.refs_7_ = f32[32,128]{1,0:T(8,128)S(1)} collective-permute-done((f32[32,128]{1,0:T(8,128)S(1)}, f32[32,128]{1,0:T(8,128)S(1)}, u32[]{:S(2)}, u32[]{:S(2)}) %collective-permute-start.4) | collective-permute-done | bytes 16416 | tf_op jit(solution)/shard_map/ppermute | solution.py:502
  32.2 8.2 %all_to_all.28 = f32[4,48,128]{2,1,0:T(8,128)S(1)} all-to-all(f32[4,48,128]{2,1,0:T(8,128)S(1)} %bitcast.9), channel_id=1, replica_groups=mesh['groups'=2,'down'=4,'cross'=2,'depth'=2] {'down'}, dimensions={0} | all-to-all | bytes 196608 | tf_op jit(solution)/shard_map/all_to_all | solution.py:491
  40.4 7.2 %field.1 = (f32[3,2,2,2,128]{4,3,2,1,0:T(2,128)}, f32[16,128]{1,0:T(8,128)S(1)}) custom-call(f32[64,128]{1,0:T(8,128)S(1)} %copy-done, f32[32,128]{1,0:T(8,128)S(1)} %collective-permute-done.refs_1_, f32[64,128]{1,0:T(8,128)S(1)} %collective-permute-done.1.refs_2_, f32[32,128]{1,0:T(8,128)S(1)} %collective-permute-done.2.refs_3_, f32[384,128]{1,0:T(8,128)S(1)} %bitcast.6, ...), custom_call_target="tpu_custom_call" | custom-call | tf_op jit(solution)/shard_map/field/pallas_call | solution.py:593
  47.6 0.0 collective-permute-start.8
  47.6 2.9 %collective-permute-start.7 = (f32[16,128]{1,0:T(8,128)S(1)}, f32[16,128]{1,0:T(8,128)S(1)}, u32[]{:S(2)}, u32[]{:S(2)}) collective-permute-start(f32[16,128]{1,0:T(8,128)S(1)} %get-tuple-element.21), channel_id=1, source_target_pairs={{0,2},{1,3},{2,0},{3,1},{4,6},{5,7},{6,4},{7,5},{8,10},{9,11},{10,... | collective-permute-start | bytes 24584 | tf_op jit(solution)/shard_map/ppermute | solution.py:547
  50.4 0.1 collective-permute-start.6
  50.5 0.1 collective-permute-done.8
  50.6 1.5 %collective-permute-done.7 = f32[16,128]{1,0:T(8,128)S(1)} collective-permute-done((f32[16,128]{1,0:T(8,128)S(1)}, f32[16,128]{1,0:T(8,128)S(1)}, u32[]{:S(2)}, u32[]{:S(2)}) %collective-permute-start.7) | collective-permute-done | bytes 8224 | tf_op jit(solution)/shard_map/ppermute | solution.py:547
  52.1 0.0 collective-permute-done.6
  52.1 0.0 copy-start.1
  52.2 8.2 %all_to_all.29.parts = f32[4,16,128]{2,1,0:T(8,128)S(1)} all-to-all(f32[4,16,128]{2,1,0:T(8,128)S(1)} %broadcast_in_dim.3), channel_id=1, replica_groups=mesh['groups'=2,'down'=4,'cross'=2,'depth'=2] {'down'}, dimensions={0} | all-to-all | bytes 65536 | tf_op jit(solution)/shard_map/all_to_all | solution.py:603
  60.4 0.0 copy-done.1
  60.4 1.5 %library.1 = (f32[2,2,2]{2,1,0:T(2,128)}, f32[48,48]{1,0:T(8,128)}, f32[1,48]{1,0:T(1,128)}) custom-call(f32[48]{0:T(128)S(1)} %copy-done.1, f32[4,16,128]{2,1,0:T(8,128)S(1)} %all_to_all.29.parts), custom_call_target="tpu_custom_call" | custom-call | tf_op jit(solution)/shard_map/library/pallas_call | solution.py:604
  (17 shorter events, 0.1 us)
Async XLA Ops:
  2.7 7.3 %collective-permute-start.2 = (f32[32,128]{1,0:T(8,128)}, f32[32,128]{1,0:T(8,128)S(1)}, u32[]{:S(2)}, u32[]{:S(2)}) collective-permute-start(f32[32,128]{1,0:T(8,128)} %get-tuple-element.16), channel_id=1, source_target_pairs={{0,3},{1,2},{2,1},{3,0},{4,7},{5,6},{6,5},{7,4},{8,11},{9,10},{10,... | collective-permute-start | bytes 49160 | tf_op jit(solution)/shard_map/ppermute | solution.py:503
  5.2 1.7 %collective-permute-start = (f32[32,128]{1,0:T(8,128)}, f32[32,128]{1,0:T(8,128)S(1)}, u32[]{:S(2)}, u32[]{:S(2)}) collective-permute-start(f32[32,128]{1,0:T(8,128)} %get-tuple-element.16), channel_id=1, source_target_pairs={{0,1},{1,0},{2,3},{3,2},{4,5},{5,4},{6,7},{7,6},{8,9},{9,8},{10,11... | collective-permute-start | bytes 49160 | tf_op jit(solution)/shard_map/ppermute | solution.py:500
  5.8 4.1 %collective-permute-start.1 = (f32[64,128]{1,0:T(8,128)}, f32[64,128]{1,0:T(8,128)S(1)}, u32[]{:S(2)}, u32[]{:S(2)}) collective-permute-start(f32[64,128]{1,0:T(8,128)} %get-tuple-element.15.refs_0_), channel_id=1, source_target_pairs={{0,2},{2,0},{1,3},{3,1},{4,6},{6,4},{5,7},{7,5},{8,10},{10,8},{9,1... | collective-permute-start | bytes 98312 | tf_op jit(solution)/shard_map/ppermute | solution.py:502
  10.1 11.5 %copy-start = (f32[64,128]{1,0:T(8,128)S(1)}, f32[64,128]{1,0:T(8,128)}, u32[]{:S(2)}) copy-start(f32[64,128]{1,0:T(8,128)} %get-tuple-element.15.refs_0_) | copy-start | bytes 98308
  27.5 3.1 %collective-permute-start.5 = (f32[16,128]{1,0:T(8,128)S(1)}, f32[16,128]{1,0:T(8,128)S(1)}, u32[]{:S(2)}, u32[]{:S(2)}) collective-permute-start(f32[16,128]{1,0:T(8,128)S(1)} %get-tuple-element.19), channel_id=1, source_target_pairs={{0,3},{1,2},{2,1},{3,0},{4,7},{5,6},{6,5},{7,4},{8,11},{9,10},{10,... | collective-permute-start | bytes 24584 | tf_op jit(solution)/shard_map/ppermute | solution.py:503
  27.5 3.1 %collective-permute-start.3 = (f32[16,128]{1,0:T(8,128)S(1)}, f32[16,128]{1,0:T(8,128)S(1)}, u32[]{:S(2)}, u32[]{:S(2)}) collective-permute-start(f32[16,128]{1,0:T(8,128)S(1)} %get-tuple-element.19), channel_id=1, source_target_pairs={{0,1},{1,0},{2,3},{3,2},{4,5},{5,4},{6,7},{7,6},{8,9},{9,8},{10,11... | collective-permute-start | bytes 24584 | tf_op jit(solution)/shard_map/ppermute | solution.py:500
  28.3 3.7 %collective-permute-start.4 = (f32[32,128]{1,0:T(8,128)S(1)}, f32[32,128]{1,0:T(8,128)S(1)}, u32[]{:S(2)}, u32[]{:S(2)}) collective-permute-start(f32[32,128]{1,0:T(8,128)S(1)} %get-tuple-element.18.refs_5_), channel_id=1, source_target_pairs={{0,2},{2,0},{1,3},{3,1},{4,6},{6,4},{5,7},{7,5},{8,10},{10,8},{9,1... | collective-permute-start | bytes 49160 | tf_op jit(solution)/shard_map/ppermute | solution.py:502
  47.6 3.1 %collective-permute-start.8 = (f32[16,128]{1,0:T(8,128)S(1)}, f32[16,128]{1,0:T(8,128)S(1)}, u32[]{:S(2)}, u32[]{:S(2)}) collective-permute-start(f32[16,128]{1,0:T(8,128)S(1)} %get-tuple-element.21), channel_id=1, source_target_pairs={{0,3},{1,2},{2,1},{3,0},{4,7},{5,6},{6,5},{7,4},{8,11},{9,10},{10,... | collective-permute-start | bytes 24584 | tf_op jit(solution)/shard_map/ppermute | solution.py:547
  47.6 4.5 %collective-permute-start.7 = (f32[16,128]{1,0:T(8,128)S(1)}, f32[16,128]{1,0:T(8,128)S(1)}, u32[]{:S(2)}, u32[]{:S(2)}) collective-permute-start(f32[16,128]{1,0:T(8,128)S(1)} %get-tuple-element.21), channel_id=1, source_target_pairs={{0,2},{1,3},{2,0},{3,1},{4,6},{5,7},{6,4},{7,5},{8,10},{9,11},{10,... | collective-permute-start | bytes 24584 | tf_op jit(solution)/shard_map/ppermute | solution.py:547
  50.4 1.7 %collective-permute-start.6 = (f32[16,128]{1,0:T(8,128)S(1)}, f32[16,128]{1,0:T(8,128)S(1)}, u32[]{:S(2)}, u32[]{:S(2)}) collective-permute-start(f32[16,128]{1,0:T(8,128)S(1)} %get-tuple-element.21), channel_id=1, source_target_pairs={{0,1},{1,0},{2,3},{3,2},{4,5},{5,4},{6,7},{7,6},{8,9},{9,8},{10,11... | collective-permute-start | bytes 24584 | tf_op jit(solution)/shard_map/ppermute | solution.py:547
  52.1 8.2 %copy-start.1 = (f32[48]{0:T(128)S(1)}, f32[48]{0:T(128)}, u32[]{:S(2)}) copy-start(f32[48]{0:T(128)} %coefficients.1) | copy-start | bytes 580
